TPU v7x, 32 devices: a whole 2x2x4 slice. The times are simulated.
32 devices in a mesh: groups: 2 (over x), wide: 16 (over z, y, core).
Axes of the slice: x: 2, y: 2, z: 4, core: 2. Of those that a mesh axis runs over, the one named last changes fastest.
Arguments:
- picture_feature_maps: bfloat16 [256, 10, 10, 1536], P(('groups', 'wide')), parts along dimension 0, may hold values from -6 to 6
- partitioned_filter_tensor: bfloat16 [3, 3, 128, 1536], replicated, may hold values from -0.1875 to 0.1875
- picture_token_layer_scaling: float32 [1536], replicated, may hold values from 0.1 to 1.9
- summary_probes: bfloat16 [64, 1536], replicated, may hold values from -6 to 6
- summary_probe_layer_scaling: float32 [1536], replicated, may hold values from 0.1 to 1.9
- asking_projection_tensor: bfloat16 [1536, 1536], P('wide'), may hold values from -0.15625 to 0.15625
- lookup_projection_tensor: bfloat16 [1536, 1536], P('wide'), may hold values from -0.15625 to 0.15625
- content_projection_tensor: bfloat16 [1536, 1536], P('wide'), may hold values from -0.15625 to 0.15625
- final_projection_tensor: bfloat16 [1536, 1536], P(None, 'wide'), may hold values from -0.15625 to 0.15625
- sharpness_coefficient: float32 [16], replicated, may hold values from 0.5 to 64
Outputs:
- attended: float32 [128, 1536], P('groups'), parts along dimension 0
- new_latents: bfloat16 [128, 1536], P('groups'), parts along dimension 0
There are 2 independent parts, one for each index of `groups`. A program takes and returns all parts, laid end to end along the dimension named above; an argument that names none is the same for every part. Nothing has to cross between parts.
All inputs are finite; a program needn't handle non-finite values.
Results may differ from a plain program's by a relative error of at most 0.004.
The roundings to bfloat16 on the way count: a program that leaves them out, or rounds other values in their place, can miss the bound.
Values may be sent and summed in bfloat16 or wider, within the bound.
A program may use at most 128 MiB of HBM per device.

v0:
```python
import functools
import math

import jax
import jax.numpy as jnp
import numpy as np
from jax import lax
from jax.experimental import pallas as pl
from jax.experimental.pallas import tpu as pltpu
from jax.sharding import PartitionSpec as P

RESIDUAL_SCALE = 0.2
EPSILON = 1e-06
LANES = 128
NT = (((1,), (1,)), ((), ()))


def layer_norm(values, gain):
    center = values - jnp.mean(values, axis=-1, keepdims=True)
    spread = jnp.mean(center * center, axis=-1, keepdims=True)
    return center * lax.rsqrt(spread + EPSILON) * gain


def window(head, breadth):
    start = head * breadth // LANES * LANES
    stop = -(-(head + 1) * breadth // LANES) * LANES
    return start, stop - start


def head_mask(head, breadth, shape):
    start, width = window(head, breadth)
    lane = lax.broadcasted_iota(jnp.int32, shape, len(shape) - 1) + start
    return (lane >= head * breadth) & (lane < (head + 1) * breadth)


def halves(values):
    high = values.astype(jnp.bfloat16)
    low = (values - high.astype(jnp.float32)).astype(jnp.bfloat16)
    return high, low


def mixer(
    n, heads,
    maps_ref, filter_ref, gain_ref, pick_ref, lat_own_ref, lat_slice_ref, probes_ref, sharp_ref,
    wq_ref, wk_ref, wv_ref, wo_ref,
    attended_ref, new_ref,
    gathered, qpart, qrecv, qall, queries, source, u_high, u_low,
    wsum, part, received, att_all, att_low, cols_all,
    plain, act, summed,
    z_send, y_send, x_send, core_send, side_send, w_recv, side_recv, swap_send, swap_recv,
):
    channels = sharp_ref.shape[1]
    breadth = channels // heads
    lats = probes_ref.shape[0]
    rows = lats // n
    shard = wk_ref.shape[0]
    line = n // 4
    me = lax.axis_index("wide")
    core = lax.rem(me, 2)
    side = lax.rem(me // 2, 2)
    at = me // 4
    team = lax.axis_index("groups")
    odd = lax.rem(team, 2)
    third = shard // 3
    piece = pl.ds(pl.multiple_of(odd * third, third), 2 * third)
    spare = pl.ds(pl.multiple_of(odd * 2 * third, third), third)
    lacking = pl.ds(pl.multiple_of((1 - odd) * 2 * third, third), third)
    weights = (wk_ref, wv_ref)

    def place(a, b, c):
        return a * 4 + b * 2 + c

    def remote(src, dst, send, recv, target):
        return pltpu.make_async_remote_copy(
            src_ref=src, dst_ref=dst, send_sem=send, recv_sem=recv,
            device_id={"wide": target}, device_id_type=pl.DeviceIdType.MESH,
        )

    def ring(k):
        return lax.rem(me + k, n)

    def back(k):
        return lax.rem(me + n - k, n)

    def loop(count, body):
        def step(k, carry):
            body(k)
            return carry
        lax.fori_loop(1, count, step, 0)

    def swap(slot, src_of, dst, target, owner):
        return remote(
            src_of(target), dst.at[owner], swap_send.at[slot, target], swap_recv.at[slot, owner], target
        )

    def swap_start(slot, src_of, dst):
        loop(n, lambda k: swap(slot, src_of, dst, ring(k), me).start())

    def swap_wait(slot, src_of, dst):
        loop(n, lambda k: swap(slot, src_of, dst, ring(k), me).wait_send())
        loop(n, lambda k: swap(slot, src_of, dst, me, back(k)).wait_recv())

    def along(w, k):
        return remote(
            weights[w].at[piece], gathered.at[w, me, piece], z_send.at[w, k], w_recv.at[w, me],
            place(lax.rem(at + k, line), side, core),
        )

    def across(w, a):
        slab = gathered.at[w, place(a, side, core), piece]
        return remote(
            slab, slab, y_send.at[w, a], w_recv.at[w, place(a, side, core)],
            place(at, 1 - side, core),
        )

    def beside(w, a, b, rows_of):
        slab = gathered.at[w, place(a, b, core), rows_of]
        return pltpu.make_async_remote_copy(
            src_ref=slab, dst_ref=slab, send_sem=x_send.at[w, a * 2 + b],
            recv_sem=side_recv.at[w, place(a, b, core)],
            device_id={"groups": team + 1 - 2 * odd, "wide": me},
            device_id_type=pl.DeviceIdType.MESH,
        )

    def over(w, a, b):
        slab = gathered.at[w, place(a, b, core), piece]
        return remote(
            slab, slab, core_send.at[w, a * 2 + b], w_recv.at[w, place(a, b, core)],
            place(at, side, 1 - core),
        )

    def over_side(w, a, b):
        slab = gathered.at[w, place(a, b, core), lacking]
        return remote(
            slab, slab, side_send.at[w, a * 2 + b], side_recv.at[w, place(a, b, core)],
            place(at, side, 1 - core),
        )

    def arrival(w, owner, rows_of, sems):
        slab = gathered.at[w, owner, rows_of]
        remote(
            slab, slab, z_send.at[w, 0], sems.at[w, owner], place(at, side, 1 - core)
        ).wait_recv()

    def line_step(w, k):
        a = lax.rem(at + line - k, line)
        arrival(w, place(a, side, core), piece, w_recv)
        across(w, a).start()
        beside(w, a, side, spare).start()
        over(w, a, side).start()

    def far_step(w, k):
        a = lax.rem(at + line - k, line)
        arrival(w, place(a, 1 - side, core), piece, w_recv)
        beside(w, a, 1 - side, spare).start()
        over(w, a, 1 - side).start()

    def side_step(w, k):
        a = lax.rem(at + line - k, line)

        @pl.when(k > 0)
        def _():
            arrival(w, place(a, side, core), lacking, side_recv)
            over_side(w, a, side).start()

        arrival(w, place(a, 1 - side, core), lacking, side_recv)
        over_side(w, a, 1 - side).start()

    def core_step(w, k):
        owner = place(k // 2, lax.rem(k, 2), 1 - core)
        arrival(w, owner, piece, w_recv)
        arrival(w, owner, lacking, side_recv)

    def finish_sends(w):
        def one(k, carry):
            a = lax.rem(at + line - k, line)
            across(w, a).wait_send()
            over(w, a, 0).wait_send()
            over(w, a, 1).wait_send()
            over_side(w, a, 0).wait_send()
            over_side(w, a, 1).wait_send()
            beside(w, a, 1 - side, spare).wait_send()

            @pl.when(k > 0)
            def _():
                beside(w, a, side, spare).wait_send()
            return carry
        loop(line, lambda k: along(w, k).wait_send())
        lax.fori_loop(0, line, one, 0)

    def each(count, body):
        def step(k, carry):
            body(k)
            return carry
        lax.fori_loop(0, count, step, 0)

    barrier = pltpu.get_barrier_semaphore()
    loop(n, lambda k: pl.semaphore_signal(
        barrier, inc=1, device_id={"wide": ring(k)}, device_id_type=pl.DeviceIdType.MESH))
    pl.semaphore_signal(
        barrier, inc=1, device_id={"groups": team + 1 - 2 * odd, "wide": me},
        device_id_type=pl.DeviceIdType.MESH)
    pl.semaphore_wait(barrier, n)

    partial = jnp.dot(lat_slice_ref[...], wq_ref[...], preferred_element_type=jnp.float32)
    for j in range(n):
        qpart[j] = partial[j * rows:(j + 1) * rows]
    qrecv[me] = qpart[me]
    swap_start(0, lambda j: qpart.at[j], qrecv)

    def send_own(w):
        gathered[w, me] = weights[w][...]
        loop(line, lambda k: along(w, k).start())
        across(w, at).start()
        over(w, at, side).start()
        over_side(w, at, side).start()

    send_own(0)
    frames, high_side, wide_side = maps_ref.shape[:3]
    group = filter_ref.shape[0] // 9
    at_once = plain.shape[0]
    pitch = plain.shape[2]
    flat = high_side * pitch
    steps = frames // at_once
    packed = pick_ref.shape[0]
    real = at_once * high_side * wide_side
    tok_count = steps * packed
    plain[...] = jnp.zeros_like(plain)
    act[...] = jnp.zeros_like(act)
    source[tok_count:] = lat_own_ref[...]

    def convolve(i):
        for f in range(at_once):
            plain[f, :, :wide_side] = maps_ref[i * at_once + f].astype(jnp.float32)
            g = jax.nn.gelu(plain[f]).reshape(flat, channels)
            act[f, 0, pitch:pitch + flat] = pltpu.roll(g, 1, 0).astype(jnp.bfloat16)
            act[f, 1, pitch:pitch + flat] = g.astype(jnp.bfloat16)
            act[f, 2, pitch:pitch + flat] = pltpu.roll(g, flat - 1, 0).astype(jnp.bfloat16)
        for c in range(channels // group):
            cut = slice(c * group, (c + 1) * group)
            taps = jnp.concatenate([
                jnp.concatenate([
                    act[f, dx, dy * pitch:dy * pitch + flat, cut]
                    for dy in range(3) for dx in range(3)
                ], axis=1)
                for f in range(at_once)
            ], axis=0)
            summed[:, cut] = jnp.dot(
                taps, filter_ref[:, cut], preferred_element_type=jnp.float32)
        normed = []
        for f in range(at_once):
            rows_of = slice(f * flat, (f + 1) * flat)
            value = plain[f].reshape(flat, channels) + RESIDUAL_SCALE * summed[rows_of]
            normed.append(layer_norm(value, gain_ref[...]).astype(jnp.bfloat16))
        dense = jnp.dot(
            pick_ref[...], jnp.concatenate(normed, axis=0), preferred_element_type=jnp.float32)
        where = pl.multiple_of(i * packed, 16)
        source[pl.ds(where, packed)] = dense.astype(jnp.bfloat16)

    def conv_and_pass(i, carry):
        convolve(i)

        @pl.when((i >= 1) & (i < line))
        def _():
            line_step(0, i)
        return carry

    lax.fori_loop(0, steps, conv_and_pass, 0)

    def pass_on(k, carry):
        line_step(0, k)
        return carry

    lax.fori_loop(min(steps, line), line, pass_on, 0)
    send_own(1)

    swap_wait(0, lambda j: qpart.at[j], qrecv)
    qall[me] = jnp.sum(qrecv[...], axis=0) * sharp_ref[...]
    swap_start(1, lambda j: qall.at[me], qall)

    each(line, lambda k: far_step(0, k))
    each(line, lambda k: side_step(0, k))
    swap_wait(1, lambda j: qall.at[me], qall)
    for j in range(n):
        queries[j * rows:(j + 1) * rows] = qall[j]
    each(n // 2, lambda k: core_step(0, k))
    loop(line, lambda k: line_step(1, k))

    per_block = max(1, min(heads, 256 // lats))
    lane = lax.broadcasted_iota(jnp.int32, (lats, LANES), 1)
    stat_max = jnp.zeros((lats, LANES), jnp.float32)
    stat_sum = jnp.zeros((lats, LANES), jnp.float32)
    for first in range(0, heads, per_block):
        folded = []
        for head in range(first, first + per_block):
            start, width = window(head, breadth)
            part_q = queries[:, start:start + width]
            part_q = jnp.where(head_mask(head, breadth, part_q.shape), part_q, 0.0)
            both = jnp.concatenate(halves(part_q), axis=0)
            look = gathered[0, :, :, start:start + width].astype(jnp.bfloat16)
            look = look.reshape(n * shard, width)
            raw = lax.dot_general(both, look, NT, preferred_element_type=jnp.float32)
            folded.append(raw[:lats] + raw[lats:])
        high, low = halves(jnp.concatenate(folded, axis=0))
        scores = lax.dot_general(high, source[...], NT, preferred_element_type=jnp.float32)
        scores += lax.dot_general(low, source[...], NT, preferred_element_type=jnp.float32)
        column = lax.broadcasted_iota(jnp.int32, scores.shape, 1)
        live = (column >= tok_count) & (column < tok_count + rows)
        for i in range(steps):
            live |= (column >= i * packed) & (column < i * packed + real)
        scores = jnp.where(live, scores, -jnp.inf)
        row_max = jnp.max(scores, axis=1, keepdims=True)
        terms = jnp.exp(scores - row_max).astype(jnp.bfloat16)
        row_sum = jnp.sum(terms.astype(jnp.float32), axis=1, keepdims=True)
        mixed = jnp.dot(terms, source[...], preferred_element_type=jnp.float32)
        high, low = halves(mixed)
        u_high[first * lats:(first + per_block) * lats] = high
        u_low[first * lats:(first + per_block) * lats] = low
        for i in range(per_block):
            stat_max = jnp.where(lane == first + i, row_max[i * lats:(i + 1) * lats], stat_max)
            stat_sum = jnp.where(lane == first + i, row_sum[i * lats:(i + 1) * lats], stat_sum)
        if first == 0:
            each(line, lambda k: far_step(1, k))
        if first == per_block:
            each(line, lambda k: side_step(1, k))
    each(n // 2, lambda k: core_step(1, k))

    wsum[...] = jnp.zeros_like(wsum)
    for head in range(heads):
        start, width = window(head, breadth)
        both = jnp.concatenate(
            [u_high[head * lats:(head + 1) * lats], u_low[head * lats:(head + 1) * lats]], axis=0
        )
        content = gathered[1, :, :, start:start + width].astype(jnp.bfloat16)
        raw = jnp.dot(both, content.reshape(n * shard, width), preferred_element_type=jnp.float32)
        raw = raw[:lats] + raw[lats:]
        wsum[:, start:start + width] += jnp.where(head_mask(head, breadth, raw.shape), raw, 0.0)
    for j in range(n):
        cut = slice(j * rows, (j + 1) * rows)
        part[j, :, :channels] = wsum[cut]
        part[j, :, channels:channels + LANES] = stat_max[cut]
        part[j, :, channels + LANES:] = stat_sum[cut]
    received[me] = part[me]
    swap_start(2, lambda j: part.at[j], received)
    swap_wait(2, lambda j: part.at[j], received)

    maxima = received[:, :, channels:channels + LANES]
    factor = jnp.exp(maxima - jnp.max(maxima, axis=0, keepdims=True))
    joint = jnp.sum(received[:, :, channels + LANES:] * factor, axis=0, keepdims=True)
    factor = factor / jnp.where(joint > 0.0, joint, 1.0)
    att_all[me] = jnp.zeros((rows, channels), jnp.float32)
    for head in range(heads):
        start, width = window(head, breadth)
        scaled = received[:, :, start:start + width] * factor[:, :, head:head + 1]
        scaled = jnp.sum(scaled, axis=0)
        keep = head_mask(head, breadth, scaled.shape)
        att_all[me, :, start:start + width] += jnp.where(keep, scaled, 0.0)
    swap_start(3, lambda j: att_all.at[me], att_all)
    swap_wait(3, lambda j: att_all.at[me], att_all)
    for j in range(n):
        wsum[j * rows:(j + 1) * rows] = att_all[j]
    att_low[...] = wsum[...].astype(jnp.bfloat16)
    cols = jnp.dot(att_low[...], wo_ref[...], preferred_element_type=jnp.float32)
    cols_all[me] = cols.astype(jnp.bfloat16)
    swap_start(4, lambda j: cols_all.at[me], cols_all)
    swap_wait(4, lambda j: cols_all.at[me], cols_all)
    wide = wo_ref.shape[1]
    for j in range(n):
        attended_ref[:, j * wide:(j + 1) * wide] = cols_all[j].astype(jnp.float32)
    new_ref[...] = (probes_ref[...].astype(jnp.float32) + attended_ref[...]).astype(jnp.bfloat16)
    finish_sends(0)
    finish_sends(1)


def per_device(
    n,
    picture_feature_maps,
    partitioned_filter_tensor,
    picture_token_layer_scaling,
    summary_probes,
    summary_probe_layer_scaling,
    asking_projection_tensor,
    lookup_projection_tensor,
    content_projection_tensor,
    final_projection_tensor,
    sharpness_coefficient,
):
    channels = picture_feature_maps.shape[3]
    heads = sharpness_coefficient.shape[0]
    breadth = channels // heads
    lats = summary_probes.shape[0]
    frames, high_side, wide_side, _ = picture_feature_maps.shape
    at_once = 2 if frames % 2 == 0 else 1
    pitch = -(-(wide_side + 1) // 16) * 16
    flat = high_side * pitch
    real = at_once * high_side * wide_side
    packed = -(-real // 16) * 16
    pick = np.zeros((packed, at_once * flat), np.float32)
    for r in range(real):
        pick[r, r // wide_side * pitch + r % wide_side] = 1.0
    filters = partitioned_filter_tensor.reshape(-1, channels)
    tok_count = frames // at_once * packed
    lat_norm = layer_norm(summary_probes.astype(jnp.float32), summary_probe_layer_scaling).astype(
        jnp.bfloat16
    )
    shard = asking_projection_tensor.shape[0]
    rows = lats // n
    me = lax.axis_index("wide")
    lat_slice = lax.dynamic_slice_in_dim(lat_norm, me * shard, shard, 1)
    lat_own = lax.dynamic_slice_in_dim(lat_norm, me * rows, rows, 0)
    extra = -(-rows // 16) * 16
    lat_own = jnp.pad(lat_own, ((0, extra - rows), (0, 0)))
    sharp = jnp.repeat(sharpness_coefficient / math.sqrt(breadth), breadth)[None, :]
    lookup, content = lookup_projection_tensor, content_projection_tensor
    wire = jnp.bfloat16 if shard % 16 == 0 else jnp.float32
    lookup, content = lookup.astype(wire), content.astype(wire)
    vmem = pl.BlockSpec(memory_space=pltpu.VMEM)
    f32, bf16 = jnp.float32, jnp.bfloat16
    width = final_projection_tensor.shape[1]
    line = n // 4
    return pl.pallas_call(
        functools.partial(mixer, n, heads),
        out_shape=(
            jax.ShapeDtypeStruct((lats, channels), f32),
            jax.ShapeDtypeStruct((lats, channels), bf16),
        ),
        in_specs=[vmem] * 12,
        out_specs=(vmem, vmem),
        scratch_shapes=[
            pltpu.VMEM((2, n, shard, channels), wire),
            pltpu.VMEM((n, rows, channels), f32),
            pltpu.VMEM((n, rows, channels), f32),
            pltpu.VMEM((n, rows, channels), f32),
            pltpu.VMEM((lats, channels), f32),
            pltpu.VMEM((tok_count + extra, channels), bf16),
            pltpu.VMEM((heads * lats, channels), bf16),
            pltpu.VMEM((heads * lats, channels), bf16),
            pltpu.VMEM((lats, channels), f32),
            pltpu.VMEM((n, rows, channels + 2 * LANES), f32),
            pltpu.VMEM((n, rows, channels + 2 * LANES), f32),
            pltpu.VMEM((n, rows, channels), f32),
            pltpu.VMEM((lats, channels), bf16),
            pltpu.VMEM((n, lats, width), bf16),
            pltpu.VMEM((at_once, high_side, pitch, channels), f32),
            pltpu.VMEM((at_once, 3, flat + 2 * pitch, channels), bf16),
            pltpu.VMEM((at_once * flat, channels), f32),
            pltpu.SemaphoreType.DMA((2, line)),
            pltpu.SemaphoreType.DMA((2, line)),
            pltpu.SemaphoreType.DMA((2, 2 * line)),
            pltpu.SemaphoreType.DMA((2, 2 * line)),
            pltpu.SemaphoreType.DMA((2, 2 * line)),
            pltpu.SemaphoreType.DMA((2, n)),
            pltpu.SemaphoreType.DMA((2, n)),
            pltpu.SemaphoreType.DMA((5, n)),
            pltpu.SemaphoreType.DMA((5, n)),
        ],
        compiler_params=pltpu.CompilerParams(
            collective_id=0, has_side_effects=True, vmem_limit_bytes=56 * 1024 * 1024
        ),
    )(
        picture_feature_maps, filters, picture_token_layer_scaling[None, :],
        jnp.asarray(pick, bf16), lat_own, lat_slice, summary_probes, sharp,
        asking_projection_tensor, lookup, content, final_projection_tensor,
    )


def solution(mesh):
    placed = (
        P(("groups", "wide"), None, None, None),
        P(),
        P(),
        P(),
        P(),
        P("wide", None),
        P("wide", None),
        P("wide", None),
        P(None, "wide"),
        P(),
    )
    return jax.shard_map(
        functools.partial(per_device, mesh.shape["wide"]),
        mesh=mesh,
        in_specs=placed,
        out_specs=(P("groups", None), P("groups", None)),
        check_vma=False,
    )
```

profile of v0, /device:TPU:0, one launch (start us, length us, event | category | flops | bytes accessed | tf_op | source)
XLA Modules:
  0.0 147.9 jit_solution(12357679908029646452)
XLA Ops:
  0.6 0.7 broadcast_multiply_fusion
  1.3 1.1 convert_reduce_fusion
  2.4 1.2 fusion.2
  3.5 1.3 broadcast_in_dim.4.gain_ref
  4.8 0.1 broadcast_in_dim.10
  4.9 0.7 broadcast_in_dim_reshape.3.sharp_ref
  5.6 1.1 fusion.4
  6.7 0.7 constant_dynamic-slice_fusion.lat_slice_ref
  7.4 0.6 pad.4.lat_own_ref
  8.0 1.9 %copy.14.wo_ref = bf16[1536,96]{1,0:T(8,128)(2,1)} copy(bf16[1536,96]{0,1:T(8,128)(2,1)} %param.19) | data formatting | bytes 589824 | tf_op args[8]
  9.9 4.5 %copy.13.maps_ref = bf16[8,10,10,1536]{3,2,1,0:T(8,128)(2,1)} copy(bf16[8,10,10,1536]{3,0,2,1:T(8,128)(2,1)} %param.11) | data formatting | bytes 4915200 | tf_op args[0]
  14.4 130.1 %shard_map.122 = (f32[64,1536]{1,0:T(8,128)}, bf16[64,1536]{1,0:T(8,128)(2,1)}) custom-call(bf16[8,10,10,1536]{3,2,1,0:T(8,128)(2,1)} %copy.13.maps_ref, bf16[1152,1536]{1,0:T(8,128)(2,1)} %bitcast.1, f32[1,1536]{1,0:T(1,128)} %broadcast_in_dim.4.gain_ref, bf16[208,320]{1,0:T(8,128)(2,1)} %constant.29.clone.pick_ref, bf16[16,1536]{1,0:T(8,128)(2,1)} %pad.4.lat_own_ref, ...), custom_call_target="tpu_custom_call" | custom-call | tf_op jit(solution)/shard_map/pallas_call | solution.py:421
  144.5 1.8 %copy.17 = f32[64,1536]{1,0:T(8,128)} copy(f32[64,1536]{1,0:T(8,128)} %get-tuple-element.4) | data formatting | bytes 786432
  146.2 1.6 %copy.18 = bf16[64,1536]{1,0:T(8,128)(2,1)} copy(bf16[64,1536]{1,0:T(8,128)(2,1)} %get-tuple-element.5) | data formatting | bytes 393216
  (3 shorter events, 0.0 us)
where the time goes:
time: 148 us
  Pallas kernels  130 us (88%)
  local copies, waits for them, and re-layouts  13.2 us (9%)
  other arithmetic  3.93 us (3%)
    pallas_call x1, Pallas kernels, per_device(): pl.pallas_call(functools.partial(mixer, n, heads), out_shape=(jax.ShapeDt...  130 us
    unnamed x4, local copies, waits for them, and re-layouts  9.8 us

commit v1 on v0

v1 whole, which is shorter than its diff:
```python
import functools
import math

import jax
import jax.numpy as jnp
import numpy as np
from jax import lax
from jax.experimental import pallas as pl
from jax.experimental.pallas import tpu as pltpu
from jax.sharding import PartitionSpec as P

RESIDUAL_SCALE = 0.2
EPSILON = 1e-06
LANES = 128
NT = (((1,), (1,)), ((), ()))


def layer_norm(values, gain):
    center = values - jnp.mean(values, axis=-1, keepdims=True)
    spread = jnp.mean(center * center, axis=-1, keepdims=True)
    return center * lax.rsqrt(spread + EPSILON) * gain


def window(head, breadth):
    start = head * breadth // LANES * LANES
    stop = -(-(head + 1) * breadth // LANES) * LANES
    return start, stop - start


def head_mask(head, breadth, shape):
    start, width = window(head, breadth)
    lane = lax.broadcasted_iota(jnp.int32, shape, len(shape) - 1) + start
    return (lane >= head * breadth) & (lane < (head + 1) * breadth)


def halves(values):
    high = values.astype(jnp.bfloat16)
    low = (values - high.astype(jnp.float32)).astype(jnp.bfloat16)
    return high, low


def mixer(
    n, heads, chunks,
    maps_ref, filter_ref, gain_ref, pick_ref, lat_own_ref, lat_slice_ref, probes_ref, sharp_ref,
    wq_ref, wk_ref, wv_ref, wo_ref,
    attended_ref, new_ref,
    gathered, qpart, qcore, qrecv, qall, queries, source, u_high, u_low,
    tail, part, received, att_all, cols_all, wo_wide,
    plain, act, summed,
    z_send, z_recv, far_send, y_send, y_recv, x_send, x_recv, pair_send, pair_recv, d_send, d_recv,
    swap_send, swap_recv, hop_send, hop_recv, head_send, head_recv,
):
    channels = sharp_ref.shape[1]
    breadth = channels // heads
    lats = probes_ref.shape[0]
    rows = lats // n
    shard = wk_ref.shape[0]
    line = n // 4
    chips = n // 2
    cut = channels // chunks
    units = 2 * chunks
    split = n // heads
    few = lats // split
    me = lax.axis_index("wide")
    core = lax.rem(me, 2)
    side = lax.rem(me // 2, 2)
    at = me // 4
    chip = me // 2
    team = lax.axis_index("groups")
    odd = lax.rem(team, 2)
    third = shard // 3
    piece = pl.ds(pl.multiple_of(odd * third, third), 2 * third)
    spare = pl.ds(pl.multiple_of(odd * 2 * third, third), third)
    lacking = pl.ds(pl.multiple_of((1 - odd) * 2 * third, third), third)
    weights = (wk_ref, wv_ref)
    far = line >= 4

    def place(a, b, c):
        return a * 4 + b * 2 + c

    def remote(src, dst, send, recv, target):
        return pltpu.make_async_remote_copy(
            src_ref=src, dst_ref=dst, send_sem=send, recv_sem=recv,
            device_id={"wide": target}, device_id_type=pl.DeviceIdType.MESH,
        )

    def beside(slab, send, recv):
        return pltpu.make_async_remote_copy(
            src_ref=slab, dst_ref=slab, send_sem=send, recv_sem=recv,
            device_id={"groups": team + 1 - 2 * odd, "wide": me},
            device_id_type=pl.DeviceIdType.MESH,
        )

    def each(first, count, body):
        def step(k, carry):
            body(k)
            return carry
        lax.fori_loop(first, count, step, 0)

    def columns(t):
        return t // chunks, pl.ds(pl.multiple_of(lax.rem(t, chunks) * cut, LANES), cut)

    def slab(t, b, a, rows_of):
        w, cols = columns(t)
        return gathered.at[w, core, b, a, rows_of, cols]

    def slabs(t, b, rows_of):
        w, cols = columns(t)
        return gathered.at[w, core, b, :, rows_of, cols]

    def along(t, a):
        own = slab(t, side, at, piece)
        return remote(own, own, z_send.at[t, a], z_recv.at[t, at], place(a, side, core))

    def along_far(t, a):
        block = slab(t, side, a, piece)
        return remote(
            block, block, far_send.at[t], z_recv.at[t, a],
            place(jnp.where(a == 0, line - 1, 0), side, core))

    def across(t, b, a):
        block = slab(t, b, a, piece)
        return remote(
            block, block, y_send.at[t, a], y_recv.at[t, a], place(at, 1 - side, core))

    def aside(t, a, rows_of):
        return beside(slab(t, side, a, rows_of), x_send.at[t, a], x_recv.at[t, a])

    def aside_all(t, rows_of):
        return beside(slabs(t, 1 - side, rows_of), pair_send.at[t], pair_recv.at[t])

    def over(t, c):
        w, cols = columns(t)
        block = gathered.at[w, c, :, :, :, cols]
        return remote(
            block, block, d_send.at[t], d_recv.at[t], place(at, side, 1 - core))

    def direct(a):
        if not far:
            return a != at
        return (a != at) & (jnp.abs(a - at) != line - 1)

    def relays(a):
        if not far:
            return None
        return ((at == line - 2) & (a == 0)) | ((at == 1) & (a == line - 1))

    def nearest(k):
        low = at < (line + 1) // 2
        seen = jnp.where(low, at, line - 1 - at)
        a = jnp.where(k - 1 < seen, k - 1, k)
        return jnp.where(low, a, line - 1 - a)

    def send_own(t):
        def one(k):
            a = nearest(k)

            @pl.when(direct(a))
            def _():
                along(t, a).start()
        each(1, line, one)
        across(t, side, at).start()

    def from_line(t):
        def one(k):
            a = nearest(k)
            own = slab(t, side, a, piece)
            remote(own, own, z_send.at[t, a], z_recv.at[t, a], place(a, side, core)).wait_recv()
            if far:
                @pl.when(relays(a))
                def _():
                    along_far(t, a).start()
            across(t, side, a).start()
            aside(t, a, spare).start()
        each(1, line, one)

    def from_across(t):
        each(0, line, lambda a: across(t, 1 - side, a).wait_recv())
        aside_all(t, spare).start()

    def from_beside(t):
        each(1, line, lambda k: aside(t, nearest(k), lacking).wait_recv())
        aside_all(t, lacking).wait_recv()
        over(t, core).start()

    def advance(t):
        if isinstance(t, int):
            def when(truth, body):
                if truth:
                    body()
        else:
            def when(truth, body):
                pl.when(truth)(body)
        when(t < units, lambda: from_line(t))
        when(t + 2 < units, lambda: send_own(t + 2))
        when((t >= 1) & (t - 1 < units), lambda: from_across(t - 1))
        when((t >= 2) & (t - 2 < units), lambda: from_beside(t - 2))
        when((t >= 3) & (t - 3 < units), lambda: over(t - 3, 1 - core).wait_recv())

    def finish_sends():
        def one(t):
            def two(k):
                a = nearest(k)

                @pl.when(direct(a))
                def _():
                    along(t, a).wait_send()
                if far:
                    @pl.when(relays(a))
                    def _():
                        along_far(t, a).wait_send()
                across(t, side, a).wait_send()
                aside(t, a, spare).wait_send()
            each(1, line, two)
            across(t, side, at).wait_send()
            aside_all(t, spare).wait_send()
            over(t, core).wait_send()
        each(0, units, one)

    def peer(k):
        return lax.rem(chip + k, chips)

    def share(slot, src_of, dst, target, owner):
        return remote(
            src_of(target), dst(owner), swap_send.at[slot, target], swap_recv.at[slot, owner],
            target * 2 + core)

    def share_start(slot, src_of, dst):
        each(1, chips, lambda k: share(slot, src_of, dst, peer(k), chip).start())

    def share_wait(slot, src_of, dst):
        each(1, chips, lambda k: share(slot, src_of, dst, peer(k), chip).wait_send())
        each(1, chips, lambda k: share(slot, src_of, dst, chip, peer(k)).wait_recv())

    def hop(slot, src, dst):
        return remote(
            src, dst, hop_send.at[slot], hop_recv.at[slot], place(at, side, 1 - core))

    def spread_start(slot, everyone):
        mine = everyone.at[core, chip]
        share_start(slot, lambda k: mine, lambda k: everyone.at[core, k])

    def spread_hop(slot, everyone):
        mine = everyone.at[core, chip]
        share_wait(slot, lambda k: mine, lambda k: everyone.at[core, k])
        hop(slot, everyone.at[core], everyone.at[core]).start()

    def spread_wait(slot, everyone):
        hop(slot, everyone.at[core], everyone.at[core]).wait_send()
        hop(slot, everyone.at[1 - core], everyone.at[1 - core]).wait_recv()

    barrier = pltpu.get_barrier_semaphore()
    each(1, n, lambda k: pl.semaphore_signal(
        barrier, inc=1, device_id={"wide": lax.rem(me + k, n)},
        device_id_type=pl.DeviceIdType.MESH))
    pl.semaphore_signal(
        barrier, inc=1, device_id={"groups": team + 1 - 2 * odd, "wide": me},
        device_id_type=pl.DeviceIdType.MESH)
    for w in range(2):
        gathered[w, core, side, at] = weights[w][...]
    pl.semaphore_wait(barrier, n)
    send_own(0)
    partial = jnp.dot(lat_slice_ref[...], wq_ref[...], preferred_element_type=jnp.float32)
    for j in range(n):
        qpart[j // chips, j % chips] = partial[j * rows:(j + 1) * rows]
    hop(3, qpart.at[1 - core], qcore).start()
    send_own(1)

    def q_pair():
        hop(3, qpart.at[1 - core], qcore).wait()
        qpart[core] += qcore[...]
        qrecv[chip] = qpart[core, chip]
        share_start(0, lambda k: qpart.at[core, k], lambda k: qrecv.at[k])

    def q_sum():
        share_wait(0, lambda k: qpart.at[core, k], lambda k: qrecv.at[k])
        qall[core, chip] = jnp.sum(qrecv[...], axis=0) * sharp_ref[...]
        spread_start(1, qall)

    def q_hop():
        spread_hop(1, qall)

    def q_done():
        spread_wait(1, qall)
        for j in range(n):
            queries[j * rows:(j + 1) * rows] = qall[j // chips, j % chips]

    wo_wide[...] = jnp.zeros_like(wo_wide)
    for head in range(heads):
        wo_wide[:, head * LANES:head * LANES + breadth] = (
            wo_ref[:, head * breadth:(head + 1) * breadth])

    frames, high_side, wide_side = maps_ref.shape[:3]
    group = filter_ref.shape[0] // 9
    at_once = plain.shape[0]
    pitch = plain.shape[2]
    flat = high_side * pitch
    steps = frames // at_once
    packed = pick_ref.shape[0]
    real = at_once * high_side * wide_side
    tok_count = steps * packed
    plain[...] = jnp.zeros_like(plain)
    act[...] = jnp.zeros_like(act)
    source[tok_count:] = lat_own_ref[...]

    def convolve(i):
        for f in range(at_once):
            plain[f, :, :wide_side] = maps_ref[i * at_once + f].astype(jnp.float32)
            g = jax.nn.gelu(plain[f]).reshape(flat, channels)
            act[f, 0, pitch:pitch + flat] = pltpu.roll(g, 1, 0).astype(jnp.bfloat16)
            act[f, 1, pitch:pitch + flat] = g.astype(jnp.bfloat16)
            act[f, 2, pitch:pitch + flat] = pltpu.roll(g, flat - 1, 0).astype(jnp.bfloat16)
        for c in range(channels // group):
            cut = slice(c * group, (c + 1) * group)
            taps = jnp.concatenate([
                jnp.concatenate([
                    act[f, dx, dy * pitch:dy * pitch + flat, cut]
                    for dy in range(3) for dx in range(3)
                ], axis=1)
                for f in range(at_once)
            ], axis=0)
            summed[:, cut] = jnp.dot(
                taps, filter_ref[:, cut], preferred_element_type=jnp.float32)
        normed = []
        for f in range(at_once):
            rows_of = slice(f * flat, (f + 1) * flat)
            value = plain[f].reshape(flat, channels) + RESIDUAL_SCALE * summed[rows_of]
            normed.append(layer_norm(value, gain_ref[...]).astype(jnp.bfloat16))
        dense = jnp.dot(
            pick_ref[...], jnp.concatenate(normed, axis=0), preferred_element_type=jnp.float32)
        where = pl.multiple_of(i * packed, 16)
        source[pl.ds(where, packed)] = dense.astype(jnp.bfloat16)

    def conv_and_pass(i):
        convolve(i)
        pl.when(i == 0)(q_pair)
        pl.when(i == 1)(q_sum)
        pl.when(i == 2)(q_hop)
        advance(i)

    each(0, min(steps, 3), conv_and_pass)
    for i in range(min(steps, 3), 3):
        (q_pair, q_sum, q_hop)[i]()
        advance(i)
    for i in range(3, steps):
        convolve(i)
    q_done()
    advance(3)

    per_block = heads // chunks
    lane = lax.broadcasted_iota(jnp.int32, (lats, LANES), 1)

    def weight(w, window_of):
        return jnp.concatenate(
            [gathered[w, j % 2, j // 2 % 2, j // 4, :, window_of] for j in range(n)], axis=0
        ).astype(jnp.bfloat16)

    def attend(first):
        folded = []
        for head in range(first, first + per_block):
            start, width = window(head, breadth)
            part_q = queries[:, start:start + width]
            part_q = jnp.where(head_mask(head, breadth, part_q.shape), part_q, 0.0)
            both = jnp.concatenate(halves(part_q), axis=0)
            look = weight(0, slice(start, start + width))
            raw = lax.dot_general(both, look, NT, preferred_element_type=jnp.float32)
            folded.append(raw[:lats] + raw[lats:])
        high, low = halves(jnp.concatenate(folded, axis=0))
        scores = lax.dot_general(high, source[...], NT, preferred_element_type=jnp.float32)
        scores += lax.dot_general(low, source[...], NT, preferred_element_type=jnp.float32)
        column = lax.broadcasted_iota(jnp.int32, scores.shape, 1)
        live = (column >= tok_count) & (column < tok_count + rows)
        for i in range(steps):
            live |= (column >= i * packed) & (column < i * packed + real)
        scores = jnp.where(live, scores, -jnp.inf)
        row_max = jnp.max(scores, axis=1, keepdims=True)
        terms = jnp.exp(scores - row_max).astype(jnp.bfloat16)
        row_sum = jnp.sum(terms.astype(jnp.float32), axis=1, keepdims=True)
        mixed = jnp.dot(terms, source[...], preferred_element_type=jnp.float32)
        high, low = halves(mixed)
        u_high[first * lats:(first + per_block) * lats] = high
        u_low[first * lats:(first + per_block) * lats] = low
        for i in range(per_block):
            kept = jnp.zeros((lats, LANES), jnp.float32)
            spot = breadth
            for value in (row_max, row_sum):
                rest = value[i * lats:(i + 1) * lats]
                for _ in range(3):
                    top = rest.astype(jnp.bfloat16).astype(jnp.float32)
                    kept = jnp.where(lane == spot, top, kept)
                    rest = rest - top
                    spot += 1
            tail[first + i] = kept

    def project(first):
        for head in range(first, first + per_block):
            start, width = window(head, breadth)
            both = jnp.concatenate(
                [u_high[head * lats:(head + 1) * lats], u_low[head * lats:(head + 1) * lats]],
                axis=0)
            content = weight(1, slice(start, start + width))
            raw = jnp.dot(both, content, preferred_element_type=jnp.float32)
            raw = raw[:lats] + raw[lats:]
            shift = head * breadth - start
            if shift:
                raw = pltpu.roll(raw, width - shift, 1)
            raw = jnp.where(lane < breadth, raw[:, :LANES], tail[head])
            part[head] = raw.astype(jnp.bfloat16)
            for s in range(split):
                to_head(head * split + s, head, s)

    def head_copy(target, head, s, owner):
        return remote(
            part.at[head, s * few:(s + 1) * few], received.at[owner],
            head_send.at[target], head_recv.at[owner], target)

    def to_head(target, head, s):
        @pl.when(me != target)
        def _():
            head_copy(target, head, s, me).start()

        @pl.when(me == target)
        def _():
            received[me] = part[head, s * few:(s + 1) * few]

    for q in range(chunks):
        attend(q * per_block)
        advance(4 + q)
    for q in range(chunks):
        project(q * per_block)
        if q < chunks - 1:
            advance(4 + chunks + q)

    each(1, n, lambda k: head_copy(me, 0, 0, lax.rem(me + k, n)).wait_recv())
    got = received[...].astype(jnp.float32)

    def number(spot):
        return got[:, :, spot:spot + 1] + got[:, :, spot + 1:spot + 2] + got[:, :, spot + 2:spot + 3]

    maxima = number(breadth)
    factor = jnp.exp(maxima - jnp.max(maxima, axis=0, keepdims=True))
    joint = jnp.sum(number(breadth + 3) * factor, axis=0)
    whole = jnp.sum(got * factor, axis=0) / joint
    narrow = lax.broadcasted_iota(jnp.int32, whole.shape, 1) < breadth
    att_all[core, chip] = jnp.where(narrow, whole, 0.0).astype(jnp.bfloat16)
    spread_start(2, att_all)
    spread_hop(2, att_all)
    spread_wait(2, att_all)
    joined = jnp.concatenate([
        jnp.concatenate([
            att_all[(head * split + s) % 2, (head * split + s) // 2] for s in range(split)
        ], axis=0)
        for head in range(heads)
    ], axis=1)
    cols = lax.dot_general(joined, wo_wide[...], NT, preferred_element_type=jnp.float32)
    cols_all[core, chip] = cols.astype(jnp.bfloat16)
    spread_start(4, cols_all)
    spread_hop(4, cols_all)
    spread_wait(4, cols_all)
    wide = wo_ref.shape[0]
    for j in range(n):
        attended_ref[:, j * wide:(j + 1) * wide] = cols_all[j % 2, j // 2].astype(jnp.float32)
    new_ref[...] = (probes_ref[...].astype(jnp.float32) + attended_ref[...]).astype(jnp.bfloat16)
    for target in range(n):
        @pl.when(me != target)
        def _(target=target):
            head_copy(target, target // split, target % split, me).wait_send()
    finish_sends()


def per_device(
    n,
    picture_feature_maps,
    partitioned_filter_tensor,
    picture_token_layer_scaling,
    summary_probes,
    summary_probe_layer_scaling,
    asking_projection_tensor,
    lookup_projection_tensor,
    content_projection_tensor,
    final_projection_tensor,
    sharpness_coefficient,
):
    channels = picture_feature_maps.shape[3]
    heads = sharpness_coefficient.shape[0]
    breadth = channels // heads
    lats = summary_probes.shape[0]
    frames, high_side, wide_side, _ = picture_feature_maps.shape
    at_once = 2 if frames % 2 == 0 else 1
    pitch = -(-(wide_side + 1) // 16) * 16
    flat = high_side * pitch
    real = at_once * high_side * wide_side
    packed = -(-real // 16) * 16
    pick = np.zeros((packed, at_once * flat), np.float32)
    for r in range(real):
        pick[r, r // wide_side * pitch + r % wide_side] = 1.0
    filters = partitioned_filter_tensor.reshape(-1, channels)
    tok_count = frames // at_once * packed
    lat_norm = layer_norm(summary_probes.astype(jnp.float32), summary_probe_layer_scaling).astype(
        jnp.bfloat16
    )
    shard = asking_projection_tensor.shape[0]
    rows = lats // n
    me = lax.axis_index("wide")
    lat_slice = lax.dynamic_slice_in_dim(lat_norm, me * shard, shard, 1)
    lat_own = lax.dynamic_slice_in_dim(lat_norm, me * rows, rows, 0)
    extra = -(-rows // 16) * 16
    lat_own = jnp.pad(lat_own, ((0, extra - rows), (0, 0)))
    sharp = jnp.repeat(sharpness_coefficient / math.sqrt(breadth), breadth)[None, :]
    lookup, content = lookup_projection_tensor, content_projection_tensor
    wire = jnp.bfloat16 if shard % 16 == 0 else jnp.float32
    lookup, content = lookup.astype(wire), content.astype(wire)
    vmem = pl.BlockSpec(memory_space=pltpu.VMEM)
    f32, bf16 = jnp.float32, jnp.bfloat16
    width = final_projection_tensor.shape[1]
    line = n // 4
    chips = n // 2
    chunks = 4
    units = 2 * chunks
    few = lats * heads // n
    return pl.pallas_call(
        functools.partial(mixer, n, heads, chunks),
        out_shape=(
            jax.ShapeDtypeStruct((lats, channels), f32),
            jax.ShapeDtypeStruct((lats, channels), bf16),
        ),
        in_specs=[vmem] * 12,
        out_specs=(vmem, vmem),
        scratch_shapes=[
            pltpu.VMEM((2, 2, 2, line, shard, channels), wire),
            pltpu.VMEM((2, chips, rows, channels), f32),
            pltpu.VMEM((chips, rows, channels), f32),
            pltpu.VMEM((chips, rows, channels), f32),
            pltpu.VMEM((2, chips, rows, channels), f32),
            pltpu.VMEM((lats, channels), f32),
            pltpu.VMEM((tok_count + extra, channels), bf16),
            pltpu.VMEM((heads * lats, channels), bf16),
            pltpu.VMEM((heads * lats, channels), bf16),
            pltpu.VMEM((heads, lats, LANES), f32),
            pltpu.VMEM((heads, lats, LANES), bf16),
            pltpu.VMEM((n, few, LANES), bf16),
            pltpu.VMEM((2, chips, few, LANES), bf16),
            pltpu.VMEM((2, chips, lats, width), bf16),
            pltpu.VMEM((width, heads * LANES), bf16),
            pltpu.VMEM((at_once, high_side, pitch, channels), f32),
            pltpu.VMEM((at_once, 3, flat + 2 * pitch, channels), bf16),
            pltpu.VMEM((at_once * flat, channels), f32),
            pltpu.SemaphoreType.DMA((units, line)),
            pltpu.SemaphoreType.DMA((units, line)),
            pltpu.SemaphoreType.DMA((units,)),
            pltpu.SemaphoreType.DMA((units, line)),
            pltpu.SemaphoreType.DMA((units, line)),
            pltpu.SemaphoreType.DMA((units, line)),
            pltpu.SemaphoreType.DMA((units, line)),
            pltpu.SemaphoreType.DMA((units,)),
            pltpu.SemaphoreType.DMA((units,)),
            pltpu.SemaphoreType.DMA((units,)),
            pltpu.SemaphoreType.DMA((units,)),
            pltpu.SemaphoreType.DMA((5, chips)),
            pltpu.SemaphoreType.DMA((5, chips)),
            pltpu.SemaphoreType.DMA((5,)),
            pltpu.SemaphoreType.DMA((5,)),
            pltpu.SemaphoreType.DMA((n,)),
            pltpu.SemaphoreType.DMA((n,)),
        ],
        compiler_params=pltpu.CompilerParams(
            collective_id=0, has_side_effects=True, vmem_limit_bytes=56 * 1024 * 1024
        ),
    )(
        picture_feature_maps, filters, picture_token_layer_scaling[None, :],
        jnp.asarray(pick, bf16), lat_own, lat_slice, summary_probes, sharp,
        asking_projection_tensor, lookup, content, final_projection_tensor.T,
    )


def solution(mesh):
    placed = (
        P(("groups", "wide"), None, None, None),
        P(),
        P(),
        P(),
        P(),
        P("wide", None),
        P("wide", None),
        P("wide", None),
        P(None, "wide"),
        P(),
    )
    return jax.shard_map(
        functools.partial(per_device, mesh.shape["wide"]),
        mesh=mesh,
        in_specs=placed,
        out_specs=(P("groups", None), P("groups", None)),
        check_vma=False,
    )
```

time: 148 us -> 102 us (0.69)
  Pallas kernels: 130 us -> 86.2 us
  local copies, waits for them, and re-layouts: 13.2 us -> 11.3 us
    pallas_call x1, Pallas kernels: 130 us -> 86.2 us  [per_device(): pl.pallas_call(functools.partial(mixer, n, heads, chunks), out_shape=(jax...]
    unnamed x4 -> x3, local copies, waits for them, and re-layouts: 9.8 us -> 7.91 us
where the time goes in v1:
time: 102 us
  Pallas kernels  86.2 us (85%)
  local copies, waits for them, and re-layouts  11.3 us (11%)
  other arithmetic  3.93 us (4%)
    pallas_call x1, Pallas kernels, per_device(): pl.pallas_call(functools.partial(mixer, n, heads, chunks), out_shape=(jax...  86.2 us
    unnamed x3, local copies, waits for them, and re-layouts  7.91 us

profile of v1, /device:TPU:0, one launch (start us, length us, event | category | flops | bytes accessed | tf_op | source)
XLA Modules:
  0.0 102.1 jit_solution(15928449367666104322)
XLA Ops:
  0.6 0.7 broadcast_multiply_fusion
  1.3 1.1 %convert_reduce_fusion = f32[64]{0:T(128)S(1)} fusion(bf16[64,1536]{1,0:T(8,128)(2,1)} %probes_ref.1), kind=kLoop, calls=%fused_computation.1 | loop fusion | flops 196544 | bytes 196864 | tf_op jit(solution)/shard_map/reduce_sum | solution.py:19
  2.4 1.2 %fusion.2 = f32[64]{0:T(128)S(1)} fusion(bf16[64,1536]{1,0:T(8,128)(2,1)} %probes_ref.1, f32[64]{0:T(128)S(1)} %broadcast_multiply_fusion.1), kind=kLoop, calls=%fused_computation.4 | loop fusion | flops 393152 | bytes 197120 | tf_op jit(solution)/shard_map/reduce_sum | solution.py:20
  3.5 1.3 %broadcast_in_dim.4.gain_ref = f32[1,1536]{1,0:T(1,128)} reshape(f32[1536]{0:T(1024)} %param.13) | data formatting | bytes 12288 | tf_op jit(solution)/shard_map/broadcast_in_dim | solution.py:570
  4.8 0.1 broadcast_in_dim.10
  4.9 0.7 broadcast_in_dim_reshape.3.sharp_ref
  5.6 1.1 %fusion.4 = bf16[64,1536]{1,0:T(8,128)(2,1)S(1)} fusion(bf16[64,1536]{1,0:T(8,128)(2,1)} %probes_ref.1, f32[1536]{0:T(1024)} %param.15, f32[64]{0:T(128)S(1)} %add_rsqrt_fusion, f32[64]{0:T(128)S(1)} %broadcast_multiply_fusion.1), kind=kLoop, calls=%fused_computation.6 | loop fusion | flops 491520 | bytes 399872 | tf_op jit(solution)/shard_map/convert_element_type | solution.py:499
  6.7 0.7 constant_dynamic-slice_fusion.lat_slice_ref
  7.4 0.6 pad.4.lat_own_ref
  8.0 4.5 %copy.13.maps_ref = bf16[8,10,10,1536]{3,2,1,0:T(8,128)(2,1)} copy(bf16[8,10,10,1536]{3,0,2,1:T(8,128)(2,1)} %param.11) | data formatting | bytes 4915200 | tf_op args[0]
  12.5 86.2 %shard_map.122 = (f32[64,1536]{1,0:T(8,128)}, bf16[64,1536]{1,0:T(8,128)(2,1)}) custom-call(bf16[8,10,10,1536]{3,2,1,0:T(8,128)(2,1)} %copy.13.maps_ref, bf16[1152,1536]{1,0:T(8,128)(2,1)} %bitcast.2, f32[1,1536]{1,0:T(1,128)} %broadcast_in_dim.4.gain_ref, bf16[208,320]{1,0:T(8,128)(2,1)} %constant.29.clone.pick_ref, bf16[16,1536]{1,0:T(8,128)(2,1)} %pad.4.lat_own_ref, ...), custom_call_target="tpu_custom_call" | custom-call | tf_op jit(solution)/shard_map/pallas_call | solution.py:521
  98.7 1.8 %copy.16 = f32[64,1536]{1,0:T(8,128)} copy(f32[64,1536]{1,0:T(8,128)} %get-tuple-element.4) | data formatting | bytes 786432
  100.5 1.6 %copy.17 = bf16[64,1536]{1,0:T(8,128)(2,1)} copy(bf16[64,1536]{1,0:T(8,128)(2,1)} %get-tuple-element.5) | data formatting | bytes 393216
  (3 shorter events, 0.0 us)

commit v2 on v1

--- a/solution.py
+++ b/solution.py
@@ -3,7 +3,6 @@
 
 import jax
 import jax.numpy as jnp
-import numpy as np
 from jax import lax
 from jax.experimental import pallas as pl
 from jax.experimental.pallas import tpu as pltpu
@@ -12,6 +11,7 @@
 RESIDUAL_SCALE = 0.2
 EPSILON = 1e-06
 LANES = 128
+AHEAD = 4
 NT = (((1,), (1,)), ((), ()))
 
 
@@ -41,20 +41,21 @@
 
 def mixer(
     n, heads, chunks,
-    maps_ref, filter_ref, gain_ref, pick_ref, lat_own_ref, lat_slice_ref, probes_ref, sharp_ref,
-    wq_ref, wk_ref, wv_ref, wo_ref,
-    attended_ref, new_ref,
-    gathered, qpart, qcore, qrecv, qall, queries, source, u_high, u_low,
+    maps_hbm, filter_hbm, gain_hbm, probes_hbm, lat_gain_hbm, sharp_ref,
+    wq_hbm, wk_hbm, wv_hbm, wo_hbm,
+    attended_ref,
+    maps_ref, filter_ref, gain_ref, probes_ref, lat_gain_ref, wq_ref, wo_ref,
+    row_of, latents, wq_wide, gathered, qpart, qcore, qrecv, qall, queries, source, u_high, u_low,
     tail, part, received, att_all, cols_all, wo_wide,
-    plain, act, summed,
-    z_send, z_recv, far_send, y_send, y_recv, x_send, x_recv, pair_send, pair_recv, d_send, d_recv,
+    act, summed,
+    load, own_load, z_send, z_recv, far_send, y_send, y_recv, x_send, x_recv, pair_send, pair_recv, d_send, d_recv,
     swap_send, swap_recv, hop_send, hop_recv, head_send, head_recv,
 ):
-    channels = sharp_ref.shape[1]
+    channels = latents.shape[1]
     breadth = channels // heads
     lats = probes_ref.shape[0]
     rows = lats // n
-    shard = wk_ref.shape[0]
+    shard = wk_hbm.shape[0]
     line = n // 4
     chips = n // 2
     cut = channels // chunks
@@ -72,7 +73,7 @@
     piece = pl.ds(pl.multiple_of(odd * third, third), 2 * third)
     spare = pl.ds(pl.multiple_of(odd * 2 * third, third), third)
     lacking = pl.ds(pl.multiple_of((1 - odd) * 2 * third, third), third)
-    weights = (wk_ref, wv_ref)
+    weights = (wk_hbm, wv_hbm)
     far = line >= 4
 
     def place(a, b, c):
@@ -192,7 +193,7 @@
             def when(truth, body):
                 pl.when(truth)(body)
         when(t < units, lambda: from_line(t))
-        when(t + 2 < units, lambda: send_own(t + 2))
+        when(t + AHEAD < units, lambda: send_own(t + AHEAD))
         when((t >= 1) & (t - 1 < units), lambda: from_across(t - 1))
         when((t >= 2) & (t - 2 < units), lambda: from_beside(t - 2))
         when((t >= 3) & (t - 3 < units), lambda: over(t - 3, 1 - core).wait_recv())
@@ -249,6 +250,18 @@
         hop(slot, everyone.at[core], everyone.at[core]).wait_send()
         hop(slot, everyone.at[1 - core], everyone.at[1 - core]).wait_recv()
 
+    taken = [
+        pltpu.make_async_copy(src, dst, load.at[k])
+        for k, (src, dst) in enumerate((
+            (probes_hbm, probes_ref), (lat_gain_hbm, lat_gain_ref), (wq_hbm, wq_ref),
+            (maps_hbm, maps_ref), (gain_hbm, gain_ref), (filter_hbm, filter_ref),
+            (wo_hbm, wo_ref),
+        ))
+    ]
+    owned = [
+        pltpu.make_async_copy(weights[w], gathered.at[w, core, side, at], own_load.at[w])
+        for w in range(2)
+    ]
     barrier = pltpu.get_barrier_semaphore()
     each(1, n, lambda k: pl.semaphore_signal(
         barrier, inc=1, device_id={"wide": lax.rem(me + k, n)},
@@ -256,15 +269,37 @@
     pl.semaphore_signal(
         barrier, inc=1, device_id={"groups": team + 1 - 2 * odd, "wide": me},
         device_id_type=pl.DeviceIdType.MESH)
-    for w in range(2):
-        gathered[w, core, side, at] = weights[w][...]
+    for copy in owned + taken:
+        copy.start()
+    lanes_all = lax.broadcasted_iota(jnp.int32, (1, channels), 1)
+    sharp = jnp.zeros((1, channels), jnp.float32)
+    for head in range(heads):
+        inside = (lanes_all >= head * breadth) & (lanes_all < (head + 1) * breadth)
+        sharp = jnp.where(inside, sharp_ref[head], sharp)
+    row_of[2:3] = sharp / math.sqrt(breadth)
+    wq_wide[...] = jnp.zeros_like(wq_wide)
+    for copy in taken[:3]:
+        copy.wait()
+    for k in range(channels // LANES):
+        row_of[1:2, k * LANES:(k + 1) * LANES] = lat_gain_ref[k:k + 1]
+    latents[...] = layer_norm(
+        probes_ref[...].astype(jnp.float32), row_of[1:2]).astype(jnp.bfloat16).astype(jnp.float32)
+    deep = wq_wide.shape[0]
+    begin = pl.multiple_of(
+        jnp.minimum(me * shard // LANES * LANES, channels - deep), LANES)
+    wq_wide[pl.ds(pl.multiple_of(me * shard - begin, 8), shard)] = wq_ref[...].astype(jnp.float32)
+    partial = jnp.dot(
+        latents[:, pl.ds(begin, deep)].astype(jnp.bfloat16), wq_wide[...].astype(jnp.bfloat16),
+        preferred_element_type=jnp.float32)
+    for j in range(n):
+        qpart[j // chips, j % chips] = partial[j * rows:(j + 1) * rows]
+    for copy in owned:
+        copy.wait()
     pl.semaphore_wait(barrier, n)
     send_own(0)
-    partial = jnp.dot(lat_slice_ref[...], wq_ref[...], preferred_element_type=jnp.float32)
-    for j in range(n):
-        qpart[j // chips, j % chips] = partial[j * rows:(j + 1) * rows]
     hop(3, qpart.at[1 - core], qcore).start()
-    send_own(1)
+    for t in range(1, AHEAD):
+        send_own(t)
 
     def q_pair():
         hop(3, qpart.at[1 - core], qcore).wait()
@@ -274,7 +309,7 @@
 
     def q_sum():
         share_wait(0, lambda k: qpart.at[core, k], lambda k: qrecv.at[k])
-        qall[core, chip] = jnp.sum(qrecv[...], axis=0) * sharp_ref[...]
+        qall[core, chip] = jnp.sum(qrecv[...], axis=0) * row_of[2:3]
         spread_start(1, qall)
 
     def q_hop():
@@ -285,65 +320,78 @@
         for j in range(n):
             queries[j * rows:(j + 1) * rows] = qall[j // chips, j % chips]
 
+    pairs = maps_ref.shape[0]
+    frames = maps_ref.shape[2]
+    high = act.shape[0] - 2
+    half = act.shape[1] - 1
+    group = filter_ref.shape[0] // 9
+    tok_count = pairs * 2 * frames
+    first_own = me * rows // 8 * 8
+
+    act[0] = jnp.zeros(act.shape[1:], jnp.bfloat16)
+    act[high + 1] = jnp.zeros(act.shape[1:], jnp.bfloat16)
+    act[:, 0, 0] = jnp.zeros((high + 2, frames, channels), jnp.bfloat16)
+    act[:, half, 1] = jnp.zeros((high + 2, frames, channels), jnp.bfloat16)
+    own_rows = latents[pl.ds(pl.multiple_of(first_own, 8), 8)]
+    source[tok_count:] = jnp.concatenate(
+        [own_rows, jnp.zeros_like(own_rows)], axis=0).astype(jnp.bfloat16)
+    taken[3].wait()
+
+    def activate(i):
+        g = jax.nn.gelu(maps_ref[i].astype(jnp.float32)).astype(jnp.bfloat16)
+        y, p = i // half, lax.rem(i, half)
+        act[y + 1, p, 1] = g[0]
+        act[y + 1, p + 1, 0] = g[1]
+
+    each(0, pairs, activate)
+    taken[4].wait()
+    taken[5].wait()
+    for k in range(channels // LANES):
+        row_of[0:1, k * LANES:(k + 1) * LANES] = gain_ref[k:k + 1]
+
+    def convolve(c):
+        lanes = pl.ds(pl.multiple_of(c * group, LANES), group)
+        taps = jnp.concatenate([
+            act[dy:dy + high, j // 2:j // 2 + half, j % 2, :, lanes].reshape(-1, group)
+            for dy in range(3) for j in range(4)
+        ], axis=1)
+        none = jnp.zeros((group, group), jnp.bfloat16)
+
+        def tap(dy, dx):
+            if not 0 <= dx < 3:
+                return none
+            return filter_ref[(dy * 3 + dx) * group:(dy * 3 + dx + 1) * group, lanes]
+
+        kernel = jnp.concatenate([
+            jnp.concatenate([tap(dy, j), tap(dy, j - 1)], axis=1)
+            for dy in range(3) for j in range(4)
+        ], axis=0)
+        both = jnp.dot(taps, kernel, preferred_element_type=jnp.float32)
+        both = both.reshape(pairs, frames, 2 * group)
+        summed[:, 0, :, lanes] = both[:, :, :group]
+        summed[:, 1, :, lanes] = both[:, :, group:]
+
+    def normalize(i):
+        value = maps_ref[i].astype(jnp.float32) + RESIDUAL_SCALE * summed[i]
+        value = layer_norm(value.reshape(2 * frames, channels), row_of[0:1])
+        where = pl.multiple_of(i * 2 * frames, 16)
+        source[pl.ds(where, 2 * frames)] = value.astype(jnp.bfloat16)
+
+    parts = channels // group
+    each(0, parts // 2, convolve)
+    q_pair()
+    advance(0)
+    each(parts // 2, parts, convolve)
+    q_sum()
+    advance(1)
+    each(0, pairs, normalize)
+    q_hop()
+    advance(2)
+    taken[6].wait()
     wo_wide[...] = jnp.zeros_like(wo_wide)
     for head in range(heads):
         wo_wide[:, head * LANES:head * LANES + breadth] = (
             wo_ref[:, head * breadth:(head + 1) * breadth])
-
-    frames, high_side, wide_side = maps_ref.shape[:3]
-    group = filter_ref.shape[0] // 9
-    at_once = plain.shape[0]
-    pitch = plain.shape[2]
-    flat = high_side * pitch
-    steps = frames // at_once
-    packed = pick_ref.shape[0]
-    real = at_once * high_side * wide_side
-    tok_count = steps * packed
-    plain[...] = jnp.zeros_like(plain)
-    act[...] = jnp.zeros_like(act)
-    source[tok_count:] = lat_own_ref[...]
-
-    def convolve(i):
-        for f in range(at_once):
-            plain[f, :, :wide_side] = maps_ref[i * at_once + f].astype(jnp.float32)
-            g = jax.nn.gelu(plain[f]).reshape(flat, channels)
-            act[f, 0, pitch:pitch + flat] = pltpu.roll(g, 1, 0).astype(jnp.bfloat16)
-            act[f, 1, pitch:pitch + flat] = g.astype(jnp.bfloat16)
-            act[f, 2, pitch:pitch + flat] = pltpu.roll(g, flat - 1, 0).astype(jnp.bfloat16)
-        for c in range(channels // group):
-            cut = slice(c * group, (c + 1) * group)
-            taps = jnp.concatenate([
-                jnp.concatenate([
-                    act[f, dx, dy * pitch:dy * pitch + flat, cut]
-                    for dy in range(3) for dx in range(3)
-                ], axis=1)
-                for f in range(at_once)
-            ], axis=0)
-            summed[:, cut] = jnp.dot(
-                taps, filter_ref[:, cut], preferred_element_type=jnp.float32)
-        normed = []
-        for f in range(at_once):
-            rows_of = slice(f * flat, (f + 1) * flat)
-            value = plain[f].reshape(flat, channels) + RESIDUAL_SCALE * summed[rows_of]
-            normed.append(layer_norm(value, gain_ref[...]).astype(jnp.bfloat16))
-        dense = jnp.dot(
-            pick_ref[...], jnp.concatenate(normed, axis=0), preferred_element_type=jnp.float32)
-        where = pl.multiple_of(i * packed, 16)
-        source[pl.ds(where, packed)] = dense.astype(jnp.bfloat16)
-
-    def conv_and_pass(i):
-        convolve(i)
-        pl.when(i == 0)(q_pair)
-        pl.when(i == 1)(q_sum)
-        pl.when(i == 2)(q_hop)
-        advance(i)
-
-    each(0, min(steps, 3), conv_and_pass)
-    for i in range(min(steps, 3), 3):
-        (q_pair, q_sum, q_hop)[i]()
-        advance(i)
-    for i in range(3, steps):
-        convolve(i)
     q_done()
     advance(3)
 
@@ -369,9 +417,8 @@
         scores = lax.dot_general(high, source[...], NT, preferred_element_type=jnp.float32)
         scores += lax.dot_general(low, source[...], NT, preferred_element_type=jnp.float32)
         column = lax.broadcasted_iota(jnp.int32, scores.shape, 1)
-        live = (column >= tok_count) & (column < tok_count + rows)
-        for i in range(steps):
-            live |= (column >= i * packed) & (column < i * packed + real)
+        own = column - tok_count - (me * rows - first_own)
+        live = (column < tok_count) | ((own >= 0) & (own < rows))
         scores = jnp.where(live, scores, -jnp.inf)
         row_max = jnp.max(scores, axis=1, keepdims=True)
         terms = jnp.exp(scores - row_max).astype(jnp.bfloat16)
@@ -459,8 +506,7 @@
     spread_wait(4, cols_all)
     wide = wo_ref.shape[0]
     for j in range(n):
-        attended_ref[:, j * wide:(j + 1) * wide] = cols_all[j % 2, j // 2].astype(jnp.float32)
-    new_ref[...] = (probes_ref[...].astype(jnp.float32) + attended_ref[...]).astype(jnp.bfloat16)
+        attended_ref[:, j * wide:(j + 1) * wide] = cols_all[j % 2, j // 2]
     for target in range(n):
         @pl.when(me != target)
         def _(target=target):
@@ -481,36 +527,22 @@
     final_projection_tensor,
     sharpness_coefficient,
 ):
-    channels = picture_feature_maps.shape[3]
+    frames, high, across, channels = picture_feature_maps.shape
     heads = sharpness_coefficient.shape[0]
-    breadth = channels // heads
     lats = summary_probes.shape[0]
-    frames, high_side, wide_side, _ = picture_feature_maps.shape
-    at_once = 2 if frames % 2 == 0 else 1
-    pitch = -(-(wide_side + 1) // 16) * 16
-    flat = high_side * pitch
-    real = at_once * high_side * wide_side
-    packed = -(-real // 16) * 16
-    pick = np.zeros((packed, at_once * flat), np.float32)
-    for r in range(real):
-        pick[r, r // wide_side * pitch + r % wide_side] = 1.0
+    maps = picture_feature_maps.transpose(1, 2, 0, 3)
+    maps = maps.reshape(high * across // 2, 2, frames, channels)
     filters = partitioned_filter_tensor.reshape(-1, channels)
-    tok_count = frames // at_once * packed
-    lat_norm = layer_norm(summary_probes.astype(jnp.float32), summary_probe_layer_scaling).astype(
-        jnp.bfloat16
-    )
+    tok_count = frames * high * across
     shard = asking_projection_tensor.shape[0]
     rows = lats // n
-    me = lax.axis_index("wide")
-    lat_slice = lax.dynamic_slice_in_dim(lat_norm, me * shard, shard, 1)
-    lat_own = lax.dynamic_slice_in_dim(lat_norm, me * rows, rows, 0)
-    extra = -(-rows // 16) * 16
-    lat_own = jnp.pad(lat_own, ((0, extra - rows), (0, 0)))
-    sharp = jnp.repeat(sharpness_coefficient / math.sqrt(breadth), breadth)[None, :]
+    extra = 16
     lookup, content = lookup_projection_tensor, content_projection_tensor
     wire = jnp.bfloat16 if shard % 16 == 0 else jnp.float32
     lookup, content = lookup.astype(wire), content.astype(wire)
+    anywhere = pl.BlockSpec(memory_space=pl.ANY)
     vmem = pl.BlockSpec(memory_space=pltpu.VMEM)
+    smem = pl.BlockSpec(memory_space=pltpu.SMEM)
     f32, bf16 = jnp.float32, jnp.bfloat16
     width = final_projection_tensor.shape[1]
     line = n // 4
@@ -518,15 +550,22 @@
     chunks = 4
     units = 2 * chunks
     few = lats * heads // n
-    return pl.pallas_call(
+    attended = pl.pallas_call(
         functools.partial(mixer, n, heads, chunks),
-        out_shape=(
-            jax.ShapeDtypeStruct((lats, channels), f32),
-            jax.ShapeDtypeStruct((lats, channels), bf16),
-        ),
-        in_specs=[vmem] * 12,
-        out_specs=(vmem, vmem),
+        out_shape=jax.ShapeDtypeStruct((lats, channels), bf16),
+        in_specs=[anywhere] * 5 + [smem] + [anywhere] * 4,
+        out_specs=vmem,
         scratch_shapes=[
+            pltpu.VMEM(maps.shape, bf16),
+            pltpu.VMEM(filters.shape, bf16),
+            pltpu.VMEM((channels // LANES, LANES), f32),
+            pltpu.VMEM((lats, channels), bf16),
+            pltpu.VMEM((channels // LANES, LANES), f32),
+            pltpu.VMEM((shard, channels), bf16),
+            pltpu.VMEM((width, channels), bf16),
+            pltpu.VMEM((8, channels), f32),
+            pltpu.VMEM((lats, channels), f32),
+            pltpu.VMEM((2 * LANES, channels), f32),
             pltpu.VMEM((2, 2, 2, line, shard, channels), wire),
             pltpu.VMEM((2, chips, rows, channels), f32),
             pltpu.VMEM((chips, rows, channels), f32),
@@ -542,9 +581,10 @@
             pltpu.VMEM((2, chips, few, LANES), bf16),
             pltpu.VMEM((2, chips, lats, width), bf16),
             pltpu.VMEM((width, heads * LANES), bf16),
-            pltpu.VMEM((at_once, high_side, pitch, channels), f32),
-            pltpu.VMEM((at_once, 3, flat + 2 * pitch, channels), bf16),
-            pltpu.VMEM((at_once * flat, channels), f32),
+            pltpu.VMEM((high + 2, across // 2 + 1, 2, frames, channels), bf16),
+            pltpu.VMEM((high * across // 2, 2, frames, channels), f32),
+            pltpu.SemaphoreType.DMA((7,)),
+            pltpu.SemaphoreType.DMA((2,)),
             pltpu.SemaphoreType.DMA((units, line)),
             pltpu.SemaphoreType.DMA((units, line)),
             pltpu.SemaphoreType.DMA((units,)),
@@ -567,10 +607,11 @@
             collective_id=0, has_side_effects=True, vmem_limit_bytes=56 * 1024 * 1024
         ),
     )(
-        picture_feature_maps, filters, picture_token_layer_scaling[None, :],
-        jnp.asarray(pick, bf16), lat_own, lat_slice, summary_probes, sharp,
+        maps, filters, picture_token_layer_scaling.reshape(-1, LANES), summary_probes,
+        summary_probe_layer_scaling.reshape(-1, LANES), sharpness_coefficient,
         asking_projection_tensor, lookup, content, final_projection_tensor.T,
-    )
+    ).astype(f32)
+    return attended, (summary_probes.astype(f32) + attended).astype(bf16)
 
 
 def solution(mesh):

time: 102 us -> 99.3 us (0.974)
  local copies, waits for them, and re-layouts: 11.3 us -> 0.01 us
  Pallas kernels: 86.2 us -> 96.7 us
  other arithmetic: 3.93 us -> 1.79 us
    pallas_call x1, Pallas kernels: 86.2 us -> 96.7 us  [per_device(): pl.pallas_call(functools.partial(mixer, n, heads, chunks), out_shape=jax....]
    unnamed x3 -> x2, local copies, waits for them, and re-layouts: 7.91 us -> 0.01 us
    reduce_sum x2 -> x0, other arithmetic: 2.2 us -> none  [the longest x1 1.15 us: layer_norm(): spread = jnp.mean(center * center, axis=-1, keepdims=True)]
    broadcast_in_dim x2 -> x0, local copies, waits for them, and re-layouts: 1.36 us -> none  [the longest x1 1.3 us: per_device(): picture_token_layer_scaling[None, :]]
where the time goes in v2:
time: 99.3 us; the launch traced here: 99.1 us
  Pallas kernels  96.7 us (97%)
  other arithmetic  1.79 us (2%)
    pallas_call x1, Pallas kernels, per_device(): pl.pallas_call(functools.partial(mixer, n, heads, chunks), out_shape=jax....  96.7 us

profile of v2, /device:TPU:0, one launch (start us, length us, event | category | flops | bytes accessed | tf_op | source)
XLA Modules:
  0.0 99.1 jit_solution(5980845965236200815)
XLA Ops:
  0.6 0.0 copy-start
  0.6 96.7 %shard_map.113 = bf16[64,1536]{1,0:T(8,128)(2,1)} custom-call(bf16[50,2,8,1536]{3,2,1,0:T(8,128)(2,1)} %bitcast.8, bf16[1152,1536]{1,0:T(8,128)(2,1)} %bitcast.7, f32[12,128]{1,0:T(8,128)} %bitcast.10, bf16[64,1536]{1,0:T(8,128)(2,1)} %probes_hbm.1, f32[12,128]{1,0:T(8,128)} %bitcast.11, f32[16]{0:T(128)} %sharp_ref.1, bf16[96,1536]{1,0:T(8,128)(2,1)} %wq_hbm.1, ...), custom_call_target="tpu_custom_call" | custom-call | tf_op jit(solution)/shard_map/pallas_call | solution.py:553
  97.3 0.0 copy-done
  97.3 1.8 %add_convert_fusion = (bf16[64,1536]{1,0:T(8,128)(2,1)}, f32[64,1536]{1,0:T(8,128)}) fusion(bf16[64,1536]{1,0:T(8,128)(2,1)S(1)} %copy-done, bf16[64,1536]{1,0:T(8,128)(2,1)} %shard_map.113), kind=kLoop, calls=%fused_computation | loop fusion | flops 393216 | bytes 983040 | tf_op jit(solution)/shard_map/convert_element_type | solution.py:614
Async XLA Ops:
  0.6 96.7 %copy-start = (bf16[64,1536]{1,0:T(8,128)(2,1)S(1)}, bf16[64,1536]{1,0:T(8,128)(2,1)}, u32[]{:S(2)}) copy-start(bf16[64,1536]{1,0:T(8,128)(2,1)} %probes_hbm.1) | copy-start | bytes 589828

commit v3 on v2

--- a/solution.py
+++ b/solution.py
@@ -11,7 +11,7 @@
 RESIDUAL_SCALE = 0.2
 EPSILON = 1e-06
 LANES = 128
-AHEAD = 4
+AHEAD = 3
 NT = (((1,), (1,)), ((), ()))
 
 
@@ -40,7 +40,7 @@
 
 
 def mixer(
-    n, heads, chunks,
+    n, heads, chunks, blocks,
     maps_hbm, filter_hbm, gain_hbm, probes_hbm, lat_gain_hbm, sharp_ref,
     wq_hbm, wk_hbm, wv_hbm, wo_hbm,
     attended_ref,
@@ -48,7 +48,7 @@
     row_of, latents, wq_wide, gathered, qpart, qcore, qrecv, qall, queries, source, u_high, u_low,
     tail, part, received, att_all, cols_all, wo_wide,
     act, summed,
-    load, own_load, z_send, z_recv, far_send, y_send, y_recv, x_send, x_recv, pair_send, pair_recv, d_send, d_recv,
+    load, own_load, sent, z_recv, y_recv, x_recv, pair_recv, d_recv,
     swap_send, swap_recv, hop_send, hop_recv, head_send, head_recv,
 ):
     channels = latents.shape[1]
@@ -74,7 +74,8 @@
     spare = pl.ds(pl.multiple_of(odd * 2 * third, third), third)
     lacking = pl.ds(pl.multiple_of((1 - odd) * 2 * third, third), third)
     weights = (wk_hbm, wv_hbm)
-    far = line >= 4
+    assert line >= 4
+    far = True
 
     def place(a, b, c):
         return a * 4 + b * 2 + c
@@ -105,36 +106,40 @@
         w, cols = columns(t)
         return gathered.at[w, core, b, a, rows_of, cols]
 
-    def slabs(t, b, rows_of):
+    def slabs(t, b, count, rows_of):
         w, cols = columns(t)
-        return gathered.at[w, core, b, :, rows_of, cols]
+        return gathered.at[w, core, b, :count, rows_of, cols]
 
     def along(t, a):
         own = slab(t, side, at, piece)
-        return remote(own, own, z_send.at[t, a], z_recv.at[t, at], place(a, side, core))
+        return remote(own, own, sent.at[0], z_recv.at[t, at], place(a, side, core))
 
     def along_far(t, a):
         block = slab(t, side, a, piece)
         return remote(
-            block, block, far_send.at[t], z_recv.at[t, a],
+            block, block, sent.at[0], z_recv.at[t, a],
             place(jnp.where(a == 0, line - 1, 0), side, core))
 
-    def across(t, b, a):
-        block = slab(t, b, a, piece)
-        return remote(
-            block, block, y_send.at[t, a], y_recv.at[t, a], place(at, 1 - side, core))
-
-    def aside(t, a, rows_of):
-        return beside(slab(t, side, a, rows_of), x_send.at[t, a], x_recv.at[t, a])
+    def over_side(block, recv):
+        return remote(block, block, sent.at[1], recv, place(at, 1 - side, core))
+
+    def across_own(b):
+        return over_side(gathered.at[:, core, b, at, piece], y_recv.at[units])
+
+    def across(t, a):
+        return over_side(slab(t, side, a, piece), y_recv.at[t])
+
+    def aside(t, a):
+        return beside(slab(t, side, a, spare), sent.at[2], x_recv.at[t])
 
     def aside_all(t, rows_of):
-        return beside(slabs(t, 1 - side, rows_of), pair_send.at[t], pair_recv.at[t])
+        return beside(slabs(t, 1 - side, line, rows_of), sent.at[3], pair_recv.at[t])
 
     def over(t, c):
         w, cols = columns(t)
         block = gathered.at[w, c, :, :, :, cols]
         return remote(
-            block, block, d_send.at[t], d_recv.at[t], place(at, side, 1 - core))
+            block, block, sent.at[4], d_recv.at[t], place(at, side, 1 - core))
 
     def direct(a):
         if not far:
@@ -160,27 +165,28 @@
             def _():
                 along(t, a).start()
         each(1, line, one)
-        across(t, side, at).start()
 
     def from_line(t):
         def one(k):
             a = nearest(k)
             own = slab(t, side, a, piece)
-            remote(own, own, z_send.at[t, a], z_recv.at[t, a], place(a, side, core)).wait_recv()
+            remote(own, own, sent.at[0], z_recv.at[t, a], place(a, side, core)).wait_recv()
             if far:
                 @pl.when(relays(a))
                 def _():
                     along_far(t, a).start()
-            across(t, side, a).start()
-            aside(t, a, spare).start()
+            across(t, a).start()
+            aside(t, a).start()
         each(1, line, one)
 
     def from_across(t):
-        each(0, line, lambda a: across(t, 1 - side, a).wait_recv())
+        if isinstance(t, int) and t == 0:
+            across_own(1 - side).wait_recv()
+        over_side(slabs(t, 1 - side, line - 1, piece), y_recv.at[t]).wait_recv()
         aside_all(t, spare).start()
 
     def from_beside(t):
-        each(1, line, lambda k: aside(t, nearest(k), lacking).wait_recv())
+        beside(slabs(t, side, line - 1, lacking), sent.at[2], x_recv.at[t]).wait_recv()
         aside_all(t, lacking).wait_recv()
         over(t, core).start()
 
@@ -199,39 +205,32 @@
         when((t >= 3) & (t - 3 < units), lambda: over(t - 3, 1 - core).wait_recv())
 
     def finish_sends():
-        def one(t):
-            def two(k):
-                a = nearest(k)
-
-                @pl.when(direct(a))
-                def _():
-                    along(t, a).wait_send()
-                if far:
-                    @pl.when(relays(a))
-                    def _():
-                        along_far(t, a).wait_send()
-                across(t, side, a).wait_send()
-                aside(t, a, spare).wait_send()
-            each(1, line, two)
-            across(t, side, at).wait_send()
-            aside_all(t, spare).wait_send()
-            over(t, core).wait_send()
-        each(0, units, one)
+        def done(k, block):
+            remote(block, block, sent.at[k], z_recv.at[0, 0], place(at, side, 1 - core)).wait_send()
+
+        done(0, gathered.at[:, core, side, :line - 2, piece])
+        end = (at == 0) | (at == line - 1)
+        pl.when(jnp.logical_not(end))(lambda: done(0, gathered.at[:, core, side, 0, piece]))
+        pl.when((at == 1) | (at == line - 2))(
+            lambda: done(0, gathered.at[:, core, side, 0, piece]))
+        done(1, gathered.at[:, core, side, :, piece])
+        done(2, gathered.at[:, core, side, :line - 1, spare])
+        done(3, gathered.at[:, core, side, :, spare])
+        done(4, gathered.at[:, core])
 
     def peer(k):
         return lax.rem(chip + k, chips)
 
-    def share(slot, src_of, dst, target, owner):
+    def share(slot, src, dst, target):
         return remote(
-            src_of(target), dst(owner), swap_send.at[slot, target], swap_recv.at[slot, owner],
-            target * 2 + core)
+            src, dst, swap_send.at[slot], swap_recv.at[slot], target * 2 + core)
 
     def share_start(slot, src_of, dst):
-        each(1, chips, lambda k: share(slot, src_of, dst, peer(k), chip).start())
-
-    def share_wait(slot, src_of, dst):
-        each(1, chips, lambda k: share(slot, src_of, dst, peer(k), chip).wait_send())
-        each(1, chips, lambda k: share(slot, src_of, dst, chip, peer(k)).wait_recv())
+        each(1, chips, lambda k: share(slot, src_of(peer(k)), dst, peer(k)).start())
+
+    def share_wait(slot, most):
+        share(slot, most, most, peer(1)).wait_send()
+        share(slot, most, most, peer(1)).wait_recv()
 
     def hop(slot, src, dst):
         return remote(
@@ -239,11 +238,10 @@
 
     def spread_start(slot, everyone):
         mine = everyone.at[core, chip]
-        share_start(slot, lambda k: mine, lambda k: everyone.at[core, k])
+        share_start(slot, lambda k: mine, mine)
 
     def spread_hop(slot, everyone):
-        mine = everyone.at[core, chip]
-        share_wait(slot, lambda k: mine, lambda k: everyone.at[core, k])
+        share_wait(slot, everyone.at[core, :chips - 1])
         hop(slot, everyone.at[core], everyone.at[core]).start()
 
     def spread_wait(slot, everyone):
@@ -271,6 +269,11 @@
         device_id_type=pl.DeviceIdType.MESH)
     for copy in owned + taken:
         copy.start()
+    for copy in owned:
+        copy.wait()
+    pl.semaphore_wait(barrier, n)
+    send_own(0)
+    across_own(side).start()
     lanes_all = lax.broadcasted_iota(jnp.int32, (1, channels), 1)
     sharp = jnp.zeros((1, channels), jnp.float32)
     for head in range(heads):
@@ -293,22 +296,16 @@
         preferred_element_type=jnp.float32)
     for j in range(n):
         qpart[j // chips, j % chips] = partial[j * rows:(j + 1) * rows]
-    for copy in owned:
-        copy.wait()
-    pl.semaphore_wait(barrier, n)
-    send_own(0)
     hop(3, qpart.at[1 - core], qcore).start()
-    for t in range(1, AHEAD):
-        send_own(t)
 
     def q_pair():
         hop(3, qpart.at[1 - core], qcore).wait()
         qpart[core] += qcore[...]
         qrecv[chip] = qpart[core, chip]
-        share_start(0, lambda k: qpart.at[core, k], lambda k: qrecv.at[k])
+        share_start(0, lambda k: qpart.at[core, k], qrecv.at[chip])
 
     def q_sum():
-        share_wait(0, lambda k: qpart.at[core, k], lambda k: qrecv.at[k])
+        share_wait(0, qrecv.at[:chips - 1])
         qall[core, chip] = jnp.sum(qrecv[...], axis=0) * row_of[2:3]
         spread_start(1, qall)
 
@@ -335,6 +332,9 @@
     own_rows = latents[pl.ds(pl.multiple_of(first_own, 8), 8)]
     source[tok_count:] = jnp.concatenate(
         [own_rows, jnp.zeros_like(own_rows)], axis=0).astype(jnp.bfloat16)
+    q_pair()
+    for t in range(1, AHEAD):
+        send_own(t)
     taken[3].wait()
 
     def activate(i):
@@ -378,24 +378,31 @@
         source[pl.ds(where, 2 * frames)] = value.astype(jnp.bfloat16)
 
     parts = channels // group
+    together = 5 if pairs % 5 == 0 else 1
+
+    def normalize_some(i):
+        for k in range(together):
+            normalize(i * together + k)
+
+    advance(0)
     each(0, parts // 2, convolve)
-    q_pair()
-    advance(0)
+    advance(1)
+    q_sum()
     each(parts // 2, parts, convolve)
-    q_sum()
-    advance(1)
-    each(0, pairs, normalize)
-    q_hop()
     advance(2)
+    each(0, pairs // together // 2, normalize_some)
+    advance(3)
+    each(pairs // together // 2, pairs // together, normalize_some)
     taken[6].wait()
     wo_wide[...] = jnp.zeros_like(wo_wide)
     for head in range(heads):
         wo_wide[:, head * LANES:head * LANES + breadth] = (
             wo_ref[:, head * breadth:(head + 1) * breadth])
+    q_hop()
+    advance(4)
     q_done()
-    advance(3)
-
-    per_block = heads // chunks
+
+    per_block = heads // blocks
     lane = lax.broadcasted_iota(jnp.int32, (lats, LANES), 1)
 
     def weight(w, window_of):
@@ -459,7 +466,7 @@
     def head_copy(target, head, s, owner):
         return remote(
             part.at[head, s * few:(s + 1) * few], received.at[owner],
-            head_send.at[target], head_recv.at[owner], target)
+            head_send.at[0], head_recv.at[0], target)
 
     def to_head(target, head, s):
         @pl.when(me != target)
@@ -470,15 +477,22 @@
         def _():
             received[me] = part[head, s * few:(s + 1) * few]
 
-    for q in range(chunks):
-        attend(q * per_block)
-        advance(4 + q)
-    for q in range(chunks):
-        project(q * per_block)
-        if q < chunks - 1:
-            advance(4 + chunks + q)
-
-    each(1, n, lambda k: head_copy(me, 0, 0, lax.rem(me + k, n)).wait_recv())
+    def ready(q, w):
+        return w * chunks + -(-(q + 1) * per_block * breadth // cut) + 2
+
+    step = 5
+    for w, work in enumerate((attend, project)):
+        for q in range(blocks):
+            while step <= ready(q, w):
+                advance(step)
+                step += 1
+            work(q * per_block)
+            if w == 0:
+                advance(step)
+                step += 1
+
+    most = received.at[:n - 1]
+    remote(most, most, head_send.at[0], head_recv.at[0], lax.rem(me + 1, n)).wait_recv()
     got = received[...].astype(jnp.float32)
 
     def number(spot):
@@ -507,10 +521,7 @@
     wide = wo_ref.shape[0]
     for j in range(n):
         attended_ref[:, j * wide:(j + 1) * wide] = cols_all[j % 2, j // 2]
-    for target in range(n):
-        @pl.when(me != target)
-        def _(target=target):
-            head_copy(target, target // split, target % split, me).wait_send()
+    remote(most, most, head_send.at[0], head_recv.at[0], lax.rem(me + 1, n)).wait_send()
     finish_sends()
 
 
@@ -547,11 +558,11 @@
     width = final_projection_tensor.shape[1]
     line = n // 4
     chips = n // 2
-    chunks = 4
+    chunks, blocks = 4, 4
     units = 2 * chunks
     few = lats * heads // n
     attended = pl.pallas_call(
-        functools.partial(mixer, n, heads, chunks),
+        functools.partial(mixer, n, heads, chunks, blocks),
         out_shape=jax.ShapeDtypeStruct((lats, channels), bf16),
         in_specs=[anywhere] * 5 + [smem] + [anywhere] * 4,
         out_specs=vmem,
@@ -585,23 +596,18 @@
             pltpu.VMEM((high * across // 2, 2, frames, channels), f32),
             pltpu.SemaphoreType.DMA((7,)),
             pltpu.SemaphoreType.DMA((2,)),
+            pltpu.SemaphoreType.DMA((5,)),
             pltpu.SemaphoreType.DMA((units, line)),
-            pltpu.SemaphoreType.DMA((units, line)),
-            pltpu.SemaphoreType.DMA((units,)),
-            pltpu.SemaphoreType.DMA((units, line)),
-            pltpu.SemaphoreType.DMA((units, line)),
-            pltpu.SemaphoreType.DMA((units, line)),
-            pltpu.SemaphoreType.DMA((units, line)),
+            pltpu.SemaphoreType.DMA((units + 1,)),
             pltpu.SemaphoreType.DMA((units,)),
             pltpu.SemaphoreType.DMA((units,)),
             pltpu.SemaphoreType.DMA((units,)),
-            pltpu.SemaphoreType.DMA((units,)),
-            pltpu.SemaphoreType.DMA((5, chips)),
-            pltpu.SemaphoreType.DMA((5, chips)),
             pltpu.SemaphoreType.DMA((5,)),
             pltpu.SemaphoreType.DMA((5,)),
-            pltpu.SemaphoreType.DMA((n,)),
-            pltpu.SemaphoreType.DMA((n,)),
+            pltpu.SemaphoreType.DMA((5,)),
+            pltpu.SemaphoreType.DMA((5,)),
+            pltpu.SemaphoreType.DMA((1,)),
+            pltpu.SemaphoreType.DMA((1,)),
         ],
         compiler_params=pltpu.CompilerParams(
             collective_id=0, has_side_effects=True, vmem_limit_bytes=56 * 1024 * 1024

time: 99.3 us -> 82.5 us (0.83)
  Pallas kernels: 96.7 us -> 79.9 us
    pallas_call x1, Pallas kernels: 96.7 us -> 79.9 us  [per_device(): pl.pallas_call(functools.partial(mixer, n, heads, chunks, blocks), out_sh...]
where the time goes in v3:
time: 82.5 us; the launch traced here: 82.3 us
  Pallas kernels  79.9 us (97%)
  other arithmetic  1.79 us (2%)
    pallas_call x1, Pallas kernels, per_device(): pl.pallas_call(functools.partial(mixer, n, heads, chunks, blocks), out_sh...  79.9 us
    convert_element_type x1, other arithmetic, per_device(): return (attended, (summary_probes.astype(f32) + attended).astype(bf16))  1.79 us

profile of v3, /device:TPU:0, one launch (start us, length us, event | category | flops | bytes accessed | tf_op | source)
XLA Modules:
  0.0 82.3 jit_solution(10047656354892894473)
XLA Ops:
  0.6 0.0 copy-start
  0.6 79.9 %shard_map.113 = bf16[64,1536]{1,0:T(8,128)(2,1)} custom-call(bf16[50,2,8,1536]{3,2,1,0:T(8,128)(2,1)} %bitcast.8, bf16[1152,1536]{1,0:T(8,128)(2,1)} %bitcast.7, f32[12,128]{1,0:T(8,128)} %bitcast.10, bf16[64,1536]{1,0:T(8,128)(2,1)} %probes_hbm.1, f32[12,128]{1,0:T(8,128)} %bitcast.11, f32[16]{0:T(128)} %sharp_ref.1, bf16[96,1536]{1,0:T(8,128)(2,1)} %wq_hbm.1, ...), custom_call_target="tpu_custom_call" | custom-call | tf_op jit(solution)/shard_map/pallas_call | solution.py:564
  80.5 0.0 copy-done
  80.5 1.8 %add_convert_fusion = (bf16[64,1536]{1,0:T(8,128)(2,1)}, f32[64,1536]{1,0:T(8,128)}) fusion(bf16[64,1536]{1,0:T(8,128)(2,1)S(1)} %copy-done, bf16[64,1536]{1,0:T(8,128)(2,1)} %shard_map.113), kind=kLoop, calls=%fused_computation | loop fusion | flops 393216 | bytes 983040 | tf_op jit(solution)/shard_map/convert_element_type | solution.py:620
Async XLA Ops:
  0.6 79.9 %copy-start = (bf16[64,1536]{1,0:T(8,128)(2,1)S(1)}, bf16[64,1536]{1,0:T(8,128)(2,1)}, u32[]{:S(2)}) copy-start(bf16[64,1536]{1,0:T(8,128)(2,1)} %probes_hbm.1) | copy-start | bytes 589828

commit v4 on v3

--- a/solution.py
+++ b/solution.py
@@ -60,8 +60,8 @@
     chips = n // 2
     cut = channels // chunks
     units = 2 * chunks
-    split = n // heads
-    few = lats // split
+    low_lats = lats // 2
+    few = heads * low_lats // chips
     me = lax.axis_index("wide")
     core = lax.rem(me, 2)
     side = lax.rem(me // 2, 2)
@@ -253,7 +253,7 @@
         for k, (src, dst) in enumerate((
             (probes_hbm, probes_ref), (lat_gain_hbm, lat_gain_ref), (wq_hbm, wq_ref),
             (maps_hbm, maps_ref), (gain_hbm, gain_ref), (filter_hbm, filter_ref),
-            (wo_hbm, wo_ref),
+            (wo_hbm, wo_ref.at[core]),
         ))
     ]
     owned = [
@@ -386,6 +386,8 @@
 
     advance(0)
     each(0, parts // 2, convolve)
+    taken[6].wait()
+    hop(2, wo_ref.at[core], wo_ref.at[core]).start()
     advance(1)
     q_sum()
     each(parts // 2, parts, convolve)
@@ -393,11 +395,12 @@
     each(0, pairs // together // 2, normalize_some)
     advance(3)
     each(pairs // together // 2, pairs // together, normalize_some)
-    taken[6].wait()
+    spread_wait(2, wo_ref)
     wo_wide[...] = jnp.zeros_like(wo_wide)
-    for head in range(heads):
-        wo_wide[:, head * LANES:head * LANES + breadth] = (
-            wo_ref[:, head * breadth:(head + 1) * breadth])
+    for c in range(2):
+        for head in range(heads):
+            wo_wide[c, :, head * LANES:head * LANES + breadth] = (
+                wo_ref[c, :, head * breadth:(head + 1) * breadth])
     q_hop()
     advance(4)
     q_done()
@@ -459,23 +462,24 @@
             if shift:
                 raw = pltpu.roll(raw, width - shift, 1)
             raw = jnp.where(lane < breadth, raw[:, :LANES], tail[head])
-            part[head] = raw.astype(jnp.bfloat16)
-            for s in range(split):
-                to_head(head * split + s, head, s)
-
-    def head_copy(target, head, s, owner):
-        return remote(
-            part.at[head, s * few:(s + 1) * few], received.at[owner],
-            head_send.at[0], head_recv.at[0], target)
-
-    def to_head(target, head, s):
-        @pl.when(me != target)
+            raw = raw.astype(jnp.bfloat16)
+            for c in range(2):
+                part[c, head * low_lats:(head + 1) * low_lats] = (
+                    raw[c * low_lats:(c + 1) * low_lats])
+            for k in range(head * low_lats // few, (head + 1) * low_lats // few):
+                for c in range(2):
+                    to_owner(k, c)
+
+    def to_owner(k, c):
+        own = part.at[c, k * few:(k + 1) * few]
+
+        @pl.when(me != k * 2 + c)
         def _():
-            head_copy(target, head, s, me).start()
-
-        @pl.when(me == target)
+            remote(own, received.at[me], head_send.at[0], head_recv.at[0], k * 2 + c).start()
+
+        @pl.when(me == k * 2 + c)
         def _():
-            received[me] = part[head, s * few:(s + 1) * few]
+            received[me] = part[c, k * few:(k + 1) * few]
 
     def ready(q, w):
         return w * chunks + -(-(q + 1) * per_block * breadth // cut) + 2
@@ -503,24 +507,32 @@
     joint = jnp.sum(number(breadth + 3) * factor, axis=0)
     whole = jnp.sum(got * factor, axis=0) / joint
     narrow = lax.broadcasted_iota(jnp.int32, whole.shape, 1) < breadth
-    att_all[core, chip] = jnp.where(narrow, whole, 0.0).astype(jnp.bfloat16)
-    spread_start(2, att_all)
-    spread_hop(2, att_all)
-    spread_wait(2, att_all)
-    joined = jnp.concatenate([
-        jnp.concatenate([
-            att_all[(head * split + s) % 2, (head * split + s) // 2] for s in range(split)
-        ], axis=0)
-        for head in range(heads)
-    ], axis=1)
-    cols = lax.dot_general(joined, wo_wide[...], NT, preferred_element_type=jnp.float32)
-    cols_all[core, chip] = cols.astype(jnp.bfloat16)
+    att_all[chip] = jnp.where(narrow, whole, 0.0).astype(jnp.bfloat16)
+    mine = att_all.at[chip]
+    share_start(2, lambda k: mine, mine)
+    share_wait(2, att_all.at[:chips - 1])
+    pieces = low_lats // few if few < low_lats else 1
+    heads_at = few // low_lats if few > low_lats else 1
+    joined = []
+    for head in range(heads):
+        if few >= low_lats:
+            first = head % heads_at * low_lats
+            joined.append(att_all[head // heads_at, first:first + low_lats])
+        else:
+            joined.append(jnp.concatenate(
+                [att_all[head * pieces + i] for i in range(pieces)], axis=0))
+    joined = jnp.concatenate(joined, axis=1)
+    wide = wo_ref.shape[1]
+    for c in range(2):
+        cols = lax.dot_general(joined, wo_wide[c], NT, preferred_element_type=jnp.float32)
+        cols_all[core, chip, :, c * wide:(c + 1) * wide] = cols.astype(jnp.bfloat16)
     spread_start(4, cols_all)
     spread_hop(4, cols_all)
     spread_wait(4, cols_all)
-    wide = wo_ref.shape[0]
-    for j in range(n):
-        attended_ref[:, j * wide:(j + 1) * wide] = cols_all[j % 2, j // 2]
+    for c in range(2):
+        for k in range(chips):
+            attended_ref[c * low_lats:(c + 1) * low_lats, k * 2 * wide:(k + 1) * 2 * wide] = (
+                cols_all[c, k])
     remote(most, most, head_send.at[0], head_recv.at[0], lax.rem(me + 1, n)).wait_send()
     finish_sends()
 
@@ -573,7 +585,7 @@
             pltpu.VMEM((lats, channels), bf16),
             pltpu.VMEM((channels // LANES, LANES), f32),
             pltpu.VMEM((shard, channels), bf16),
-            pltpu.VMEM((width, channels), bf16),
+            pltpu.VMEM((2, width, channels), bf16),
             pltpu.VMEM((8, channels), f32),
             pltpu.VMEM((lats, channels), f32),
             pltpu.VMEM((2 * LANES, channels), f32),
@@ -587,11 +599,11 @@
             pltpu.VMEM((heads * lats, channels), bf16),
             pltpu.VMEM((heads * lats, channels), bf16),
             pltpu.VMEM((heads, lats, LANES), f32),
-            pltpu.VMEM((heads, lats, LANES), bf16),
+            pltpu.VMEM((2, heads * lats // 2, LANES), bf16),
             pltpu.VMEM((n, few, LANES), bf16),
-            pltpu.VMEM((2, chips, few, LANES), bf16),
-            pltpu.VMEM((2, chips, lats, width), bf16),
-            pltpu.VMEM((width, heads * LANES), bf16),
+            pltpu.VMEM((chips, few, LANES), bf16),
+            pltpu.VMEM((2, chips, lats // 2, 2 * width), bf16),
+            pltpu.VMEM((2, width, heads * LANES), bf16),
             pltpu.VMEM((high + 2, across // 2 + 1, 2, frames, channels), bf16),
             pltpu.VMEM((high * across // 2, 2, frames, channels), f32),
             pltpu.SemaphoreType.DMA((7,)),

time: 82.5 us -> 81.3 us (0.985)
  Pallas kernels: 79.9 us -> 78.7 us
    pallas_call x1, Pallas kernels: 79.9 us -> 78.7 us  [per_device(): pl.pallas_call(functools.partial(mixer, n, heads, chunks, blocks), out_sh...]
where the time goes in v4:
time: 81.3 us; the launch traced here: 81.2 us
  Pallas kernels  78.7 us (97%)
  other arithmetic  1.79 us (2%)
    pallas_call x1, Pallas kernels, per_device(): pl.pallas_call(functools.partial(mixer, n, heads, chunks, blocks), out_sh...  78.7 us
    convert_element_type x1, other arithmetic, per_device(): return (attended, (summary_probes.astype(f32) + attended).astype(bf16))  1.79 us

profile of v4, /device:TPU:0, one launch (start us, length us, event | category | flops | bytes accessed | tf_op | source)
XLA Modules:
  0.0 81.2 jit_solution(3072589063433039166)
XLA Ops:
  0.6 0.0 copy-start
  0.6 78.7 %shard_map.113 = bf16[64,1536]{1,0:T(8,128)(2,1)} custom-call(bf16[50,2,8,1536]{3,2,1,0:T(8,128)(2,1)} %bitcast.8, bf16[1152,1536]{1,0:T(8,128)(2,1)} %bitcast.7, f32[12,128]{1,0:T(8,128)} %bitcast.10, bf16[64,1536]{1,0:T(8,128)(2,1)} %probes_hbm.1, f32[12,128]{1,0:T(8,128)} %bitcast.11, f32[16]{0:T(128)} %sharp_ref.1, bf16[96,1536]{1,0:T(8,128)(2,1)} %wq_hbm.1, ...), custom_call_target="tpu_custom_call" | custom-call | tf_op jit(solution)/shard_map/pallas_call | solution.py:576
  79.4 0.0 copy-done
  79.4 1.8 %add_convert_fusion = (bf16[64,1536]{1,0:T(8,128)(2,1)}, f32[64,1536]{1,0:T(8,128)}) fusion(bf16[64,1536]{1,0:T(8,128)(2,1)S(1)} %copy-done, bf16[64,1536]{1,0:T(8,128)(2,1)} %shard_map.113), kind=kLoop, calls=%fused_computation | loop fusion | flops 393216 | bytes 983040 | tf_op jit(solution)/shard_map/convert_element_type | solution.py:632
Async XLA Ops:
  0.6 78.7 %copy-start = (bf16[64,1536]{1,0:T(8,128)(2,1)S(1)}, bf16[64,1536]{1,0:T(8,128)(2,1)}, u32[]{:S(2)}) copy-start(bf16[64,1536]{1,0:T(8,128)(2,1)} %probes_hbm.1) | copy-start | bytes 589828

commit v5 on v4

--- a/solution.py
+++ b/solution.py
@@ -190,19 +190,23 @@
         aside_all(t, lacking).wait_recv()
         over(t, core).start()
 
+    def advance_line(t):
+        if t < units:
+            from_line(t)
+        if t + AHEAD < units:
+            send_own(t + AHEAD)
+
+    def advance_rest(t):
+        if 1 <= t <= units:
+            from_across(t - 1)
+        if 2 <= t <= units + 1:
+            from_beside(t - 2)
+        if 3 <= t <= units + 2:
+            over(t - 3, 1 - core).wait_recv()
+
     def advance(t):
-        if isinstance(t, int):
-            def when(truth, body):
-                if truth:
-                    body()
-        else:
-            def when(truth, body):
-                pl.when(truth)(body)
-        when(t < units, lambda: from_line(t))
-        when(t + AHEAD < units, lambda: send_own(t + AHEAD))
-        when((t >= 1) & (t - 1 < units), lambda: from_across(t - 1))
-        when((t >= 2) & (t - 2 < units), lambda: from_beside(t - 2))
-        when((t >= 3) & (t - 3 < units), lambda: over(t - 3, 1 - core).wait_recv())
+        advance_line(t)
+        advance_rest(t)
 
     def finish_sends():
         def done(k, block):
@@ -413,19 +417,21 @@
             [gathered[w, j % 2, j // 2 % 2, j // 4, :, window_of] for j in range(n)], axis=0
         ).astype(jnp.bfloat16)
 
-    def attend(first):
-        folded = []
-        for head in range(first, first + per_block):
-            start, width = window(head, breadth)
-            part_q = queries[:, start:start + width]
-            part_q = jnp.where(head_mask(head, breadth, part_q.shape), part_q, 0.0)
-            both = jnp.concatenate(halves(part_q), axis=0)
-            look = weight(0, slice(start, start + width))
-            raw = lax.dot_general(both, look, NT, preferred_element_type=jnp.float32)
-            folded.append(raw[:lats] + raw[lats:])
-        high, low = halves(jnp.concatenate(folded, axis=0))
+    def attend(first, between):
+        block = slice(first * breadth, (first + per_block) * breadth)
+        some = queries[:, block]
+        at_lane = lax.broadcasted_iota(jnp.int32, some.shape, 1)
+        asked = jnp.concatenate([
+            jnp.where((at_lane >= i * breadth) & (at_lane < (i + 1) * breadth), some, 0.0)
+            for i in range(per_block)
+        ], axis=0)
+        look = weight(0, block)
+        raw = lax.dot_general(
+            jnp.concatenate(halves(asked), axis=0), look, NT, preferred_element_type=jnp.float32)
+        high, low = halves(raw[:per_block * lats] + raw[per_block * lats:])
         scores = lax.dot_general(high, source[...], NT, preferred_element_type=jnp.float32)
         scores += lax.dot_general(low, source[...], NT, preferred_element_type=jnp.float32)
+        between()
         column = lax.broadcasted_iota(jnp.int32, scores.shape, 1)
         own = column - tok_count - (me * rows - first_own)
         live = (column < tok_count) | ((own >= 0) & (own < rows))
@@ -485,15 +491,17 @@
         return w * chunks + -(-(q + 1) * per_block * breadth // cut) + 2
 
     step = 5
-    for w, work in enumerate((attend, project)):
+    for w in range(2):
         for q in range(blocks):
             while step <= ready(q, w):
                 advance(step)
                 step += 1
-            work(q * per_block)
             if w == 0:
-                advance(step)
+                attend(q * per_block, lambda: advance_line(step))
+                advance_rest(step)
                 step += 1
+            else:
+                project(q * per_block)
 
     most = received.at[:n - 1]
     remote(most, most, head_send.at[0], head_recv.at[0], lax.rem(me + 1, n)).wait_recv()

time: 81.3 us -> 80.3 us (0.988)
  Pallas kernels: 78.7 us -> 77.7 us
    pallas_call x1, Pallas kernels: 78.7 us -> 77.7 us  [per_device(): pl.pallas_call(functools.partial(mixer, n, heads, chunks, blocks), out_sh...]
where the time goes in v5:
time: 80.3 us; the launch traced here: 80.1 us
  Pallas kernels  77.7 us (97%)
  other arithmetic  1.79 us (2%)
    pallas_call x1, Pallas kernels, per_device(): pl.pallas_call(functools.partial(mixer, n, heads, chunks, blocks), out_sh...  77.7 us
    convert_element_type x1, other arithmetic, per_device(): return (attended, (summary_probes.astype(f32) + attended).astype(bf16))  1.79 us

profile of v5, /device:TPU:0, one launch (start us, length us, event | category | flops | bytes accessed | tf_op | source)
XLA Modules:
  0.0 80.1 jit_solution(11650020191396549530)
XLA Ops:
  0.6 0.0 copy-start
  0.6 77.7 %shard_map.113 = bf16[64,1536]{1,0:T(8,128)(2,1)} custom-call(bf16[50,2,8,1536]{3,2,1,0:T(8,128)(2,1)} %bitcast.8, bf16[1152,1536]{1,0:T(8,128)(2,1)} %bitcast.7, f32[12,128]{1,0:T(8,128)} %bitcast.10, bf16[64,1536]{1,0:T(8,128)(2,1)} %probes_hbm.1, f32[12,128]{1,0:T(8,128)} %bitcast.11, f32[16]{0:T(128)} %sharp_ref.1, bf16[96,1536]{1,0:T(8,128)(2,1)} %wq_hbm.1, ...), custom_call_target="tpu_custom_call" | custom-call | tf_op jit(solution)/shard_map/pallas_call | solution.py:584
  78.3 0.0 copy-done
  78.3 1.8 %add_convert_fusion = (bf16[64,1536]{1,0:T(8,128)(2,1)}, f32[64,1536]{1,0:T(8,128)}) fusion(bf16[64,1536]{1,0:T(8,128)(2,1)S(1)} %copy-done, bf16[64,1536]{1,0:T(8,128)(2,1)} %shard_map.113), kind=kLoop, calls=%fused_computation | loop fusion | flops 393216 | bytes 983040 | tf_op jit(solution)/shard_map/convert_element_type | solution.py:640
Async XLA Ops:
  0.6 77.7 %copy-start = (bf16[64,1536]{1,0:T(8,128)(2,1)S(1)}, bf16[64,1536]{1,0:T(8,128)(2,1)}, u32[]{:S(2)}) copy-start(bf16[64,1536]{1,0:T(8,128)(2,1)} %probes_hbm.1) | copy-start | bytes 589828

commit v6 on v5

--- a/solution.py
+++ b/solution.py
@@ -417,7 +417,7 @@
             [gathered[w, j % 2, j // 2 % 2, j // 4, :, window_of] for j in range(n)], axis=0
         ).astype(jnp.bfloat16)
 
-    def attend(first, between):
+    def attend(first, early, between):
         block = slice(first * breadth, (first + per_block) * breadth)
         some = queries[:, block]
         at_lane = lax.broadcasted_iota(jnp.int32, some.shape, 1)
@@ -429,6 +429,7 @@
         raw = lax.dot_general(
             jnp.concatenate(halves(asked), axis=0), look, NT, preferred_element_type=jnp.float32)
         high, low = halves(raw[:per_block * lats] + raw[per_block * lats:])
+        early()
         scores = lax.dot_general(high, source[...], NT, preferred_element_type=jnp.float32)
         scores += lax.dot_general(low, source[...], NT, preferred_element_type=jnp.float32)
         between()
@@ -497,8 +498,8 @@
                 advance(step)
                 step += 1
             if w == 0:
-                attend(q * per_block, lambda: advance_line(step))
-                advance_rest(step)
+                attend(
+                    q * per_block, lambda: advance_line(step), lambda: advance_rest(step))
                 step += 1
             else:
                 project(q * per_block)

time: 80.3 us -> 79.8 us (level)
  no operation moved by 1% of the time
where the time goes in v6:
time: 79.8 us; the launch traced here: 79.6 us
  Pallas kernels  77.2 us (97%)
  other arithmetic  1.79 us (2%)
    pallas_call x1, Pallas kernels, per_device(): pl.pallas_call(functools.partial(mixer, n, heads, chunks, blocks), out_sh...  77.2 us
    convert_element_type x1, other arithmetic, per_device(): return (attended, (summary_probes.astype(f32) + attended).astype(bf16))  1.79 us

profile of v6, /device:TPU:0, one launch (start us, length us, event | category | flops | bytes accessed | tf_op | source)
XLA Modules:
  0.0 79.6 jit_solution(9252733400092738448)
XLA Ops:
  0.6 0.0 copy-start
  0.6 77.2 %shard_map.113 = bf16[64,1536]{1,0:T(8,128)(2,1)} custom-call(bf16[50,2,8,1536]{3,2,1,0:T(8,128)(2,1)} %bitcast.8, bf16[1152,1536]{1,0:T(8,128)(2,1)} %bitcast.7, f32[12,128]{1,0:T(8,128)} %bitcast.10, bf16[64,1536]{1,0:T(8,128)(2,1)} %probes_hbm.1, f32[12,128]{1,0:T(8,128)} %bitcast.11, f32[16]{0:T(128)} %sharp_ref.1, bf16[96,1536]{1,0:T(8,128)(2,1)} %wq_hbm.1, ...), custom_call_target="tpu_custom_call" | custom-call | tf_op jit(solution)/shard_map/pallas_call | solution.py:585
  77.8 0.0 copy-done
  77.8 1.8 %add_convert_fusion = (bf16[64,1536]{1,0:T(8,128)(2,1)}, f32[64,1536]{1,0:T(8,128)}) fusion(bf16[64,1536]{1,0:T(8,128)(2,1)S(1)} %copy-done, bf16[64,1536]{1,0:T(8,128)(2,1)} %shard_map.113), kind=kLoop, calls=%fused_computation | loop fusion | flops 393216 | bytes 983040 | tf_op jit(solution)/shard_map/convert_element_type | solution.py:641
Async XLA Ops:
  0.6 77.2 %copy-start = (bf16[64,1536]{1,0:T(8,128)(2,1)S(1)}, bf16[64,1536]{1,0:T(8,128)(2,1)}, u32[]{:S(2)}) copy-start(bf16[64,1536]{1,0:T(8,128)(2,1)} %probes_hbm.1) | copy-start | bytes 589828

commit v7 on v6

--- a/solution.py
+++ b/solution.py
@@ -11,7 +11,7 @@
 RESIDUAL_SCALE = 0.2
 EPSILON = 1e-06
 LANES = 128
-AHEAD = 3
+AHEAD = 4
 NT = (((1,), (1,)), ((), ()))
 
 

time: 79.8 us -> 83.4 us (1.045)
  Pallas kernels: 77.2 us -> 80.8 us
    pallas_call x1, Pallas kernels: 77.2 us -> 80.8 us  [per_device(): pl.pallas_call(functools.partial(mixer, n, heads, chunks, blocks), out_sh...]
where the time goes in v7:
time: 83.4 us; the launch traced here: 83.3 us
  Pallas kernels  80.8 us (97%)
  other arithmetic  1.79 us (2%)
    pallas_call x1, Pallas kernels, per_device(): pl.pallas_call(functools.partial(mixer, n, heads, chunks, blocks), out_sh...  80.8 us
    convert_element_type x1, other arithmetic, per_device(): return (attended, (summary_probes.astype(f32) + attended).astype(bf16))  1.79 us

profile of v7, /device:TPU:0, one launch (start us, length us, event | category | flops | bytes accessed | tf_op | source)
XLA Modules:
  0.0 83.3 jit_solution(5830242253382861059)
XLA Ops:
  0.6 0.0 copy-start
  0.6 80.8 %shard_map.113 = bf16[64,1536]{1,0:T(8,128)(2,1)} custom-call(bf16[50,2,8,1536]{3,2,1,0:T(8,128)(2,1)} %bitcast.8, bf16[1152,1536]{1,0:T(8,128)(2,1)} %bitcast.7, f32[12,128]{1,0:T(8,128)} %bitcast.10, bf16[64,1536]{1,0:T(8,128)(2,1)} %probes_hbm.1, f32[12,128]{1,0:T(8,128)} %bitcast.11, f32[16]{0:T(128)} %sharp_ref.1, bf16[96,1536]{1,0:T(8,128)(2,1)} %wq_hbm.1, ...), custom_call_target="tpu_custom_call" | custom-call | tf_op jit(solution)/shard_map/pallas_call | solution.py:585
  81.5 0.0 copy-done
  81.5 1.8 %add_convert_fusion = (bf16[64,1536]{1,0:T(8,128)(2,1)}, f32[64,1536]{1,0:T(8,128)}) fusion(bf16[64,1536]{1,0:T(8,128)(2,1)S(1)} %copy-done, bf16[64,1536]{1,0:T(8,128)(2,1)} %shard_map.113), kind=kLoop, calls=%fused_computation | loop fusion | flops 393216 | bytes 983040 | tf_op jit(solution)/shard_map/convert_element_type | solution.py:641
Async XLA Ops:
  0.6 80.9 %copy-start = (bf16[64,1536]{1,0:T(8,128)(2,1)S(1)}, bf16[64,1536]{1,0:T(8,128)(2,1)}, u32[]{:S(2)}) copy-start(bf16[64,1536]{1,0:T(8,128)(2,1)} %probes_hbm.1) | copy-start | bytes 589828
